TPU v7x, 256 devices: a whole 4x4x8 slice. The times are simulated.
256 devices in a mesh: walk: 16 (over y, z_hi, core), chol: 16 (over z_lo, x).
Axes of the slice: x: 4, y: 4, z: 8 (z_hi: 2, z_lo: 4; z = z_hi * 4 + z_lo), core: 2. Of those that a mesh axis runs over, the one named last changes fastest.
Arguments:
- greens: bfloat16 [512, 2, 100, 1000], P(('walk', 'chol')), may hold values from -6 to 6
- cholesky: bfloat16 [176, 2, 100, 1000], P('chol'), may hold values from -0.013671875 to 0.013671875
- fields: float32 [512, 176], P(('walk', 'chol')), may hold values from -6 to 6
- log_weight: float32 [512], P(('walk', 'chol')), may hold values from -4 to 4
- group_of: int32 [512], P(('walk', 'chol')), may hold values from 0 to 15
Outputs:
- force_bias: float32 [512, 176], P(('walk', 'chol'))
- e_coulomb: float32 [512], P(('walk', 'chol'))
- e_exchange: float32 [512], P(('walk', 'chol'))
- new_log_weight: float32 [512], P(('walk', 'chol'))
- group_share: float32 [16], replicated
All inputs are finite; a program needn't handle non-finite values.
Results may differ from a plain program's by a relative error of at most 0.0003.
Values may be sent and summed in bfloat16 or wider, within the bound.
A program may use at most 192 MiB of HBM per device.

v0:
```python
import jax
import jax.numpy as jnp
from jax import lax
from jax.sharding import PartitionSpec as P

GROUPS = 16


def local(greens, cholesky, fields, log_weight, group_of):
    walk_count = greens.shape[0]
    slab = cholesky.shape[0]
    chol_count = lax.axis_size("chol")
    root = jnp.sqrt(jnp.float32(slab * chol_count))
    half = walk_count // 2
    bias_parts = []
    exch_parts = []
    for batch in range(2):
        members = greens[batch * half : (batch + 1) * half]
        prods = jnp.einsum(
            "gsip,wsjp->wgsij",
            cholesky,
            lax.all_gather(members, "chol", axis=0, tiled=True),
            preferred_element_type=jnp.float32,
        )
        bias = jnp.einsum("wgsii->wg", prods)
        exch = jnp.einsum("wgsij,wgsji->w", prods, prods)
        bias_parts.append(lax.all_to_all(bias, "chol", split_axis=0, concat_axis=1, tiled=True))
        exch_parts.append(lax.psum_scatter(exch, "chol", scatter_dimension=0, tiled=True))
    force_bias = jnp.concatenate(bias_parts, axis=0)
    exch_sum = jnp.concatenate(exch_parts, axis=0)
    e_coulomb = jnp.sum(force_bias * force_bias, axis=1) / (2.0 * root)
    e_exchange = -exch_sum / (2.0 * root)
    importance = jnp.sum(fields * force_bias - 0.5 * force_bias * force_bias, axis=1) / root
    new_log_weight = log_weight + importance - e_coulomb - e_exchange
    onehot = (group_of[:, None] == jnp.arange(GROUPS, dtype=jnp.int32)[None, :]).astype(jnp.float32)
    local_sums = jnp.dot(jnp.exp(new_log_weight), onehot, precision=lax.Precision.HIGHEST)
    group_sums = lax.psum(local_sums, ("walk", "chol"))
    group_share = GROUPS * group_sums / jnp.sum(group_sums)
    return (force_bias, e_coulomb, e_exchange, new_log_weight, group_share)


def solution(mesh):
    in_specs = (
        P(("walk", "chol"), None, None, None),
        P("chol", None, None, None),
        P(("walk", "chol"), None),
        P(("walk", "chol")),
        P(("walk", "chol")),
    )
    out_specs = (
        P(("walk", "chol"), None),
        P(("walk", "chol")),
        P(("walk", "chol")),
        P(("walk", "chol")),
        P(),
    )
    return jax.shard_map(local, mesh=mesh, in_specs=in_specs, out_specs=out_specs, check_vma=False)
```

profile of v0, /device:TPU:1, one launch (start us, length us, event | category | flops | bytes accessed | tf_op | source)
XLA Modules:
  0.0 446.1 jit_solution(2656273283903075712)
XLA Ops:
  7.2 0.0 all-gather.3.cloned.1.call-start
  7.2 1.7 fusion.15
  8.9 0.9 copy.42
  9.8 0.0 all-gather.3.cloned.1.call-update
  9.8 0.0 all-gather.5.cloned.1.call-start
  9.8 0.9 copy.43
  10.7 0.0 all-gather.5.cloned.1.call-update
  10.7 91.1 %all-gather.3.cloned.1.call-done = bf16[16,2,100,1000]{3,2,0,1:T(8,128)(2,1)} async-done(((bf16[1,2,100,1000]{3,2,0,1:T(8,128)(2,1)}), bf16[16,2,100,1000]{3,2,0,1:T(8,128)(2,1)}) %all-gather.3.cloned.1.call-update) | async-done | bytes 6400016 | tf_op jit(solution)/shard_map/all_gather | solution.py:22
  101.8 21.3 %bitcast_reduce_fusion.1 = (f32[16,11,100,100]{2,3,1,0:T(8,128)}, f32[2,16,100,11,100]{4,2,3,1,0:T(8,128)}) fusion(bf16[11,2,100,1000,1]{3,1,2,0,4:T(2,128)(2,1)} %bitcast.44, bf16[16,2,100,1000]{3,2,0,1:T(8,128)(2,1)} %all-gather.3.cloned.1.call-done), kind=kOutput, calls=%fused_computation.5 | convolution fusion | flops 7041760256 | bytes 31920000 | tf_op jit(solution)/shard_map/gsip,wsjp->wgsij/dot_general | solution.py:19
  123.1 72.4 %all-gather.5.cloned.1.call-done = bf16[16,2,100,1000]{3,2,0,1:T(8,128)(2,1)} async-done(((bf16[1,2,100,1000]{3,2,0,1:T(8,128)(2,1)}), bf16[16,2,100,1000]{3,2,0,1:T(8,128)(2,1)}) %all-gather.5.cloned.1.call-update) | async-done | bytes 6400016 | tf_op jit(solution)/shard_map/all_gather | solution.py:22
  195.5 21.4 %bitcast_reduce_fusion = (f32[16,11,100,100]{2,3,1,0:T(8,128)}, f32[2,16,100,11,100]{4,2,3,1,0:T(8,128)}) fusion(bf16[11,2,100,1000,1]{3,1,2,0,4:T(2,128)(2,1)} %bitcast.45, bf16[16,2,100,1000]{3,2,0,1:T(8,128)(2,1)} %all-gather.5.cloned.1.call-done), kind=kOutput, calls=%fused_computation.4 | convolution fusion | flops 7041760256 | bytes 31920000 | tf_op jit(solution)/shard_map/gsip,wsjp->wgsij/dot_general | solution.py:19
  216.9 0.0 copy-start.4
  216.9 9.6 %select_reduce_fusion.1 = (f32[16,11]{1,0:T(8,128)}, f32[16,11]{1,0:T(8,128)}) fusion(f32[16,11,100,100]{2,3,1,0:T(8,128)} %get-tuple-element.17, pred[100,100]{0,1:T(8,128)(4,1)S(1)} %iota_compare_fusion, f32[16,11,100,100]{2,3,1,0:T(8,128)} %get-tuple-element.19), kind=kLoop, calls=%fused_computation.7 | loop fusion | flops 7039648 | bytes 14091408 | tf_op jit(solution)/shard_map/wgsii->wg/reduce_sum | solution.py:25
  226.5 4.7 %all-to-all-start.1 = ((f32[16,1,11]{2,1,0:T(1,128)}), f32[16,1,11]{2,1,0:T(1,128)S(1)}, u32[]{:S(2)}, u32[]{:S(2)}) async-start(f32[16,1,11]{2,1,0:T(1,128)} %bitcast.13), calls=%async_computation.1 | async-start | bytes 16384 | tf_op jit(solution)/shard_map/all_to_all | solution.py:27
  231.2 0.0 copy-done.4
  231.2 0.6 dynamic-slice
  231.8 21.0 %copy.37 = f32[16,11,100,100,2]{3,2,1,0,4:T(8,128)} copy(f32[16,11,100,100,2]{2,3,1,0,4:T(8,128)} %bitcast.43) | data formatting | bytes 28160000
  252.8 21.0 %copy.31 = f32[16,11,100,100,2]{3,2,1,0,4:T(8,128)} copy(f32[16,11,100,100,2]{2,3,1,0,4:T(8,128)} %bitcast.42) | data formatting | bytes 28160000
  273.8 0.0 all-to-all-done.1
  273.8 6.9 %all-to-all-start = ((f32[16,1,11]{2,1,0:T(1,128)}), f32[16,1,11]{2,1,0:T(1,128)S(1)}, u32[]{:S(2)}, u32[]{:S(2)}) async-start(f32[16,1,11]{2,1,0:T(1,128)} %bitcast.8), calls=%async_computation | async-start | bytes 16384 | tf_op jit(solution)/shard_map/all_to_all | solution.py:27
  280.7 0.0 copy-start
  280.8 0.0 copy-start.1
  280.8 0.0 copy-start.3
  280.8 23.9 %fusion = (f32[16]{0:T(128)S(1)}, f32[16]{0:T(128)S(1)}) fusion(f32[16,11,100,100,2]{3,2,1,0,4:T(8,128)} %copy.37, f32[2,16,100,11,100]{4,2,3,1,0:T(8,128)} %get-tuple-element.20, f32[16,11,100,100,2]{3,2,1,0,4:T(8,128)} %copy.31, f32[2,16,100,11,100]{4,2,3,1,0:T(8,128)} %get-tuple-element.18), kind=kLoop, calls=%fused_computation.1 | loop fusion | flops 14079968 | bytes 56320128 | tf_op jit(solution)/shard_map/wgsij,wgsji->w/dot_general | solution.py:26
  304.6 36.1 %all-reduce.2 = (f32[16]{0:T(128)S(1)}, f32[16]{0:T(128)S(1)}) all-reduce(f32[16]{0:T(128)S(1)} %get-tuple-element.21, f32[16]{0:T(128)S(1)} %get-tuple-element.22), channel_id=3, replica_groups=mesh['walk'=16,'chol'=16] {'chol'}, use_global_device_ids=true, to_apply=%region_6.0.clone | all-reduce | flops 32 | bytes 256
  340.7 1.2 dynamic-slice.3
  342.0 1.3 dynamic-slice.1
  343.3 0.5 broadcast.32
  343.8 0.7 reduce.10
  344.5 0.1 all_to_all.29
  344.5 0.0 all-to-all-done
  344.6 0.7 reduce.11
  345.2 0.1 all_to_all.26
  345.3 0.0 copy-done
  345.3 0.7 fusion.9
  346.1 0.0 copy-done.1
  346.1 1.9 subtract_subtract_fusion
  348.0 0.0 copy-start.2
  348.0 0.0 copy-done.3
  348.0 0.2 convolution_bitcast_fusion
  348.2 89.2 %psum.7 = f32[16]{0:T(128)S(1)} all-reduce(f32[16]{0:T(128)S(1)} %convolution_bitcast_fusion), channel_id=1, replica_groups=mesh['walk'=16,'chol'=16] {'walk','chol'}, use_global_device_ids=true, to_apply=%region_8.0 | all-reduce | flops 16 | bytes 128 | tf_op jit(solution)/shard_map/psum | solution.py:37
  437.4 0.7 reduce_sum.69
  438.0 1.2 multiply_divide_fusion
  439.2 0.0 copy-done.2
  (1 shorter events, 0.0 us)
Async XLA Ops:
  7.2 94.6 %all-gather.3.cloned.1.call-start = ((), (), s32[]{:S(2)}) async-start(), calls=%async_computation.2 | async-start | bytes 7241728 | tf_op jit(solution)/shard_map/all_gather | solution.py:22
  9.8 185.7 %all-gather.5.cloned.1.call-start = ((), (), s32[]{:S(2)}) async-start(), calls=%async_computation.3 | async-start | bytes 7241728 | tf_op jit(solution)/shard_map/all_gather | solution.py:22
  216.9 14.3 %copy-start.4 = (u32[256]{0:T(256)S(1)}, u32[256]{0:T(256)}, u32[]{:S(2)}) copy-start(u32[256]{0:T(256)} %constant.23) | copy-start | bytes 3076
  226.5 47.3 %all-to-all-start.1 = ((f32[16,1,11]{2,1,0:T(1,128)}), f32[16,1,11]{2,1,0:T(1,128)S(1)}, u32[]{:S(2)}, u32[]{:S(2)}) async-start(f32[16,1,11]{2,1,0:T(1,128)} %bitcast.13), calls=%async_computation.1 | async-start | bytes 16384 | tf_op jit(solution)/shard_map/all_to_all | solution.py:27
  273.8 70.8 %all-to-all-start = ((f32[16,1,11]{2,1,0:T(1,128)}), f32[16,1,11]{2,1,0:T(1,128)S(1)}, u32[]{:S(2)}, u32[]{:S(2)}) async-start(f32[16,1,11]{2,1,0:T(1,128)} %bitcast.8), calls=%async_computation | async-start | bytes 16384 | tf_op jit(solution)/shard_map/all_to_all | solution.py:27
  280.7 64.6 %copy-start = (f32[2,176]{1,0:T(2,128)S(1)}, f32[2,176]{1,0:T(2,128)}, u32[]{:S(2)}) copy-start(f32[2,176]{1,0:T(2,128)} %param.7) | copy-start | bytes 4228
  280.8 65.3 %copy-start.1 = (f32[2]{0:T(128)S(1)}, f32[2]{0:T(128)}, u32[]{:S(2)}) copy-start(f32[2]{0:T(128)} %param.8) | copy-start | bytes 28
  280.8 67.2 %copy-start.3 = (s32[2]{0:T(128)S(1)}, s32[2]{0:T(128)}, u32[]{:S(2)}) copy-start(s32[2]{0:T(128)} %param.9) | copy-start | bytes 28
  348.0 91.2 %copy-start.2 = (f32[2]{0:T(128)}, f32[2]{0:T(128)S(1)}, u32[]{:S(2)}) copy-start(f32[2]{0:T(128)S(1)} %get-tuple-element.11) | copy-start | bytes 28
Sparse Core Ops, SparseCore 0:
  9.9 91.8 all-gather.2
  103.6 91.8 all-gather.4
where the time goes:
time: 447 us; the launch traced here: 446 us
  waiting for transfers between devices  163 us (36%)
  blocking collectives  125 us (28%)
  local copies, waits for them, and re-layouts  49.2 us (11%)
  matrix products  42.9 us (10%)
  other arithmetic  39.4 us (9%)
  between operations  14.2 us (3%)
  starting transfers between devices  11.7 us (3%)
    all_gather x2, waiting for transfers between devices, local(): lax.all_gather(members, 'chol', axis=0, tiled=True)  163 us
    psum x1, blocking collectives, local(): group_sums = lax.psum(local_sums, ('walk', 'chol'))  89.2 us
    unnamed x17, local copies, waits for them, and re-layouts  46.8 us
    dot_general x2, matrix products, local(): jnp.einsum('gsip,wsjp->wgsij', cholesky, lax.all_gather(members, 'chol',...  42.7 us
    unnamed x1, blocking collectives  36.1 us
    dot_general x1, other arithmetic, local(): exch = jnp.einsum('wgsij,wgsji->w', prods, prods)  23.9 us
    all_to_all x2, starting transfers between devices, local(): lax.all_to_all(bias, 'chol', split_axis=0, concat_axis=1, tiled=True)  11.6 us
    reduce_sum x1, other arithmetic, local(): bias = jnp.einsum('wgsii->wg', prods)  9.64 us
  transfers between devices with their start and end apart: 4, of which 2 were waited for; matrix products, arithmetic and copies ran while one was open for 21% of the time, Pallas kernels for 0%

commit v1 on v0

v1 whole, which is shorter than its diff:
```python
import functools

import jax
import jax.numpy as jnp
import numpy as np
from jax import lax
from jax.experimental import pallas as pl
from jax.experimental.pallas import tpu as pltpu
from jax.sharding import PartitionSpec as P

GROUPS = 16
ROWS = 112
MESH = pl.DeviceIdType.MESH
HIGHEST = lax.Precision.HIGHEST

SLOTS = ((0, 0), (1, 0), (0, -1), (0, 1), (1, -1), (1, 1), (0, 2), (1, -2))


def device(x, y, z, core):
    return {"walk": (y * 2 + lax.div(z, 4)) * 2 + core, "chol": lax.rem(z, 4) * 4 + x}


def kernel(
    greens, cholesky, fields, log_weight, group_of,
    bias_out, coulomb_out, exchange_out, weight_out, share_out,
    slabs, walkers, c_pad, g_pad, prods_a, prods_b, bias_rows, exch,
    back, back_in, combined, stage_out, stage_in,
    local_sem, c_send, c_recv, g_send, g_recv, b_send, b_recv, s_send, s_recv,
):
    wi, ci = lax.axis_index("walk"), lax.axis_index("chol")
    core = lax.rem(wi, 2)
    y = lax.div(wi, 4)
    z_lo = lax.div(ci, 4)
    z = lax.rem(lax.div(wi, 2), 2) * 4 + z_lo
    x = lax.rem(ci, 4)
    spin = lax.div(y, 2)
    mate = 3 - y
    step = 1 - 2 * core

    def at_x(offset):
        return lax.rem(x + offset + 4, 4)

    def at_z(offset):
        return lax.rem(z + offset + 8, 8)

    def stage_peer(stage, r):
        if stage == 0:
            p = lax.rem(y * 4 + x + r, 16)
            return device(lax.rem(p, 4), lax.div(p, 4), z, core)
        p = lax.rem(z * 2 + core + r, 16)
        return device(x, y, lax.div(p, 2), lax.rem(p, 2))

    own_c = pltpu.make_async_copy(cholesky.at[:, spin], slabs.at[pl.ds(x * 11, 11)], local_sem.at[0])
    own_g = pltpu.make_async_copy(greens.at[:, spin], walkers.at[0], local_sem.at[1])
    own_g.start()
    own_c.start()

    barrier = pltpu.get_barrier_semaphore()

    def greet(peer):
        pl.semaphore_signal(barrier, inc=1, device_id=peer, device_id_type=MESH)

    for stage in range(2):
        def greet_stage(r, _, stage=stage):
            greet(stage_peer(stage, r))
            return 0
        lax.fori_loop(1, 16, greet_stage, 0)
    for offset in (-2, -1, 1, 2):
        greet(device(x, mate, at_z(offset), core))
    pl.semaphore_wait(barrier, 34)

    first_a, first_b = 6 * core, 6 * core + 3 + 0 * core
    parts = {"a": (first_a, 3), "b": (first_b, 2), "m": (5, 1)}
    c_copies = {}

    def c_copy(index, src, slab, part, peer):
        first, count = parts[part]
        place = slabs.at[pl.ds(slab * 11 + first, count)]
        if src is None:
            src = cholesky.at[pl.ds(first, count), spin]
        else:
            src = place
        return pltpu.make_async_remote_copy(
            src_ref=src, dst_ref=place, send_sem=c_send.at[index], recv_sem=c_recv.at[index],
            device_id=peer, device_id_type=MESH,
        )

    ahead, behind = at_x(step), at_x(-step)
    to_ahead, to_behind = device(ahead, y, z, core), device(behind, y, z, core)
    sibling = device(x, y, z, 1 - core)
    opposite = at_x(2)
    direct = [
        c_copy(0, None, x, "a", to_ahead),
        c_copy(3, None, x, "b", to_behind),
        c_copy(1, None, x, "b", to_ahead),
        c_copy(4, None, x, "a", to_behind),
        c_copy(2, None, x, "m", to_ahead),
    ]
    relay = {
        5: c_copy(5, 1, behind, "a", to_ahead),
        6: c_copy(6, 1, ahead, "b", to_behind),
        7: c_copy(7, 1, behind, "m", to_ahead),
    }
    landed = {0: (behind, "a"), 1: (behind, "b"), 2: (behind, "m"), 3: (ahead, "b"), 4: (ahead, "a"),
              5: (opposite, "a"), 6: (opposite, "b"), 7: (opposite, "m")}
    arrive = {i: c_copy(i, 1, slab, part, to_ahead) for i, (slab, part) in landed.items()}
    share = {i: c_copy(8 + i, 1, slab, part, sibling) for i, (slab, part) in landed.items()}

    their = {"a": (6 - first_a, 3), "b": (9 - first_a, 2), "m": (5, 1)}

    def from_sibling(i):
        slab, part = landed[i]
        if i < 5:
            slab = ahead if i < 3 else behind
        first, count = their[part]
        place = slabs.at[pl.ds(slab * 11 + first, count)]
        return pltpu.make_async_remote_copy(
            src_ref=place, dst_ref=place, send_sem=c_send.at[8 + i], recv_sem=c_recv.at[8 + i],
            device_id=sibling, device_id_type=MESH,
        )

    def g_copy(index, src, slot, peer):
        return pltpu.make_async_remote_copy(
            src_ref=src, dst_ref=walkers.at[slot], send_sem=g_send.at[index], recv_sem=g_recv.at[slot],
            device_id=peer, device_id_type=MESH,
        )

    own_planes, other_planes = greens.at[:, spin], greens.at[:, 1 - spin]
    g_copies = [
        g_copy(0, other_planes, 1, device(x, mate, z, core)),
        g_copy(1, own_planes, 2, device(x, y, at_z(1), core)),
        g_copy(2, own_planes, 3, device(x, y, at_z(-1), core)),
        g_copy(3, own_planes, 6, device(x, y, at_z(-2), core)),
        g_copy(4, walkers.at[1], 4, device(x, y, at_z(1), core)),
        g_copy(5, walkers.at[1], 5, device(x, y, at_z(-1), core)),
        g_copy(6, walkers.at[1], 7, device(x, y, at_z(2), core)),
    ]

    def g_wait(slot):
        g_copy(0, walkers.at[slot], slot, sibling).wait_recv()

    g_copies[0].start()
    for copy in direct[:2]:
        copy.start()
    for copy in g_copies[1:3]:
        copy.start()
    for copy in direct[2:]:
        copy.start()
    g_copies[3].start()

    zero = jnp.zeros((ROWS, 1024), jnp.bfloat16)

    def clear_c(i, _):
        c_pad[pl.ds(i * ROWS, ROWS), :] = zero
        return 0

    def clear_g(i, _):
        g_pad[i] = jnp.zeros((128, 1024), jnp.bfloat16)
        bias_rows[i] = jnp.zeros((128, 128), jnp.float32)
        exch[i] = jnp.zeros((8, 128), jnp.float32)
        return 0

    lax.fori_loop(0, 44, clear_c, 0)
    lax.fori_loop(0, 16, clear_g, 0)

    def pack_slab(slab):
        def one(i, _):
            g = slab * 11 + i
            c_pad[pl.ds(g * ROWS, 100), 0:1000] = slabs[g]
            return 0
        lax.fori_loop(0, 11, one, 0)

    def pack_walkers(slot):
        for i in range(2):
            g_pad[slot * 2 + i, 0:100, 0:1000] = walkers[slot, i]

    row = lax.broadcasted_iota(jnp.int32, (104, 128), 0)
    col = lax.broadcasted_iota(jnp.int32, (104, 128), 1)
    diagonal = row == col

    def slab_of(task):
        q = lax.div(task, 8)
        return lax.rem(x + jnp.where(q == 2, 3, jnp.where(q == 3, 2, q)), 4)

    def product(task, buf):
        slot = lax.rem(task, 8)
        lhs = c_pad[pl.ds(slab_of(task) * (11 * ROWS), 11 * ROWS), :]
        rhs = g_pad[pl.ds(slot * 2, 2)].reshape(256, 1024)
        buf[...] = lax.dot_general(lhs, rhs, (((1,), (1,)), ((), ())), preferred_element_type=jnp.float32)

    def reduce(task, buf):
        slot = lax.rem(task, 8)
        first = slab_of(task) * 11
        for h in range(2):
            total = None
            for g in range(11):
                p = buf[g * ROWS : (g + 1) * ROWS, h * 128 : (h + 1) * 128]
                turned = p.T
                q = p[:104, :ROWS] * turned[:104, :]
                part = jnp.sum(q.reshape(13, 8, ROWS), axis=0)
                total = part if total is None else total + part
                d = jnp.sum(jnp.where(diagonal, p[:104], 0.0).reshape(13, 8, 128), axis=0)
                bias_rows[slot * 2 + h, pl.ds(first + g, 1), :] = jnp.sum(d, axis=0, keepdims=True)
            exch[slot * 2 + h, :, 0:ROWS] += total

    def events(k):
        @pl.when(k == 0)
        def _():
            own_c.wait()
            own_g.wait()
            pack_slab(x)
            pack_walkers(0)
            g_wait(1)
            for copy in g_copies[4:]:
                copy.start()
            pack_walkers(1)

        @pl.when(k == 1)
        def _():
            g_wait(2)
            g_wait(3)
            pack_walkers(2)
            pack_walkers(3)
            arrive[3].wait_recv()
            relay[6].start()
            share[3].start()
            arrive[0].wait_recv()
            relay[5].start()
            share[0].start()

        @pl.when(k == 2)
        def _():
            g_wait(4)
            g_wait(5)
            pack_walkers(4)
            pack_walkers(5)
            for i in (1, 4):
                arrive[i].wait_recv()
                share[i].start()

        @pl.when(k == 3)
        def _():
            g_wait(6)
            g_wait(7)
            pack_walkers(6)
            pack_walkers(7)
            arrive[2].wait_recv()
            share[2].start()

            @pl.when(core == 0)
            def _():
                relay[7].start()

        @pl.when(k == 4)
        def _():
            for i in range(5):
                from_sibling(i).wait_recv()
            pack_slab(at_x(1))

        @pl.when(k == 8)
        def _():
            pack_slab(at_x(3))

        @pl.when(k == 10)
        def _():
            for i in (6, 5):
                arrive[i].wait_recv()
                share[i].start()

            @pl.when(core == 0)
            def _():
                arrive[7].wait_recv()
                share[7].start()

        @pl.when(k == 12)
        def _():
            for i in (6, 5):
                from_sibling(i).wait_recv()

            @pl.when(core == 1)
            def _():
                from_sibling(7).wait_recv()
            pack_slab(opposite)

    prods_b[...] = jnp.zeros_like(prods_b)

    def body(k, _):
        events(k)
        product(2 * k, prods_a)

        reduce(jnp.maximum(2 * k - 1, 0), prods_b)
        product(2 * k + 1, prods_b)
        reduce(2 * k, prods_a)
        return 0

    lax.fori_loop(0, 16, body, 0)
    reduce(jnp.int32(31), prods_b)

    for w in range(16):
        bias_rows[w, 44:45, :] = jnp.sum(exch[w], axis=0, keepdims=True)
    ones = jnp.ones((8, 128), jnp.float32)
    sums = lax.dot_general(
        ones, bias_rows[...].reshape(16 * 128, 128), (((1,), (1,)), ((), ())),
        precision=HIGHEST, preferred_element_type=jnp.float32,
    )
    for slot in range(8):
        back[slot] = sums[:, slot * 256 : (slot + 1) * 256]
    returns = []
    for slot, (other, offset) in enumerate(SLOTS):
        if slot:
            copy = pltpu.make_async_remote_copy(
                src_ref=back.at[slot], dst_ref=back_in.at[slot], send_sem=b_send.at[slot], recv_sem=b_recv.at[slot],
                device_id=device(x, mate if other else y, at_z(offset), core), device_id_type=MESH,
            )
            copy.start()
            returns.append(copy)
    for copy in returns:
        copy.wait_recv()
    own = back[0]
    for quarter, (s, t) in enumerate(((0, 1), (3, 5), (6, 7), (2, 4))):
        combined[quarter] = (own if s == 0 else back_in[s]) + back_in[t]
    lane = lax.broadcasted_iota(jnp.int32, (8, 128), 1)
    bias, exch_sum = [], []
    for w in range(2):
        spread, total = None, None
        for m in range(4):
            block = combined[lax.rem(z_lo - m + 4, 4), :, w * 128 : (w + 1) * 128]
            energy = jnp.sum(jnp.where(lane == 44, block, 0.0), axis=1, keepdims=True)
            wide = jnp.concatenate([jnp.where(lane < 44, block, 0.0), jnp.zeros((8, 128), jnp.float32)], axis=1)
            if m:
                wide = pltpu.roll(wide, 44 * m, 1)
            spread = wide if spread is None else spread + wide
            total = energy if total is None else total + energy
        bias.append(spread)
        exch_sum.append(total)
    top = lax.broadcasted_iota(jnp.int32, (8, 256), 0) == 0
    bias = jnp.where(top, bias[0], bias[1])[0:2, 0:176]
    first = lax.broadcasted_iota(jnp.int32, (2, 1), 0) == 0
    exch_sum = jnp.where(first, exch_sum[0][0:2], exch_sum[1][0:2])
    root = np.sqrt(np.float32(176))
    bias_out[...] = bias
    coulomb = jnp.sum(bias * bias, axis=1, keepdims=True) / (2.0 * root)
    exchange = -exch_sum / (2.0 * root)
    importance = jnp.sum(fields[...] * bias - 0.5 * bias * bias, axis=1, keepdims=True) / root
    weight = jnp.where(first, log_weight[0], log_weight[1]) + importance - coulomb - exchange
    member = lax.broadcasted_iota(jnp.int32, (2, 128), 1) == jnp.where(
        lax.broadcasted_iota(jnp.int32, (2, 128), 0) == 0, group_of[0], group_of[1]
    )
    group = jnp.sum(jnp.where(member, jnp.exp(weight), 0.0), axis=0, keepdims=True)

    for stage in range(2):
        me = y * 4 + x if stage == 0 else z * 2 + core
        group = jnp.broadcast_to(group, (8, 128))
        stage_out[stage] = group
        stage_in[stage, 0] = group

        def send(r, _, stage=stage):
            pltpu.make_async_remote_copy(
                src_ref=stage_out.at[stage], dst_ref=stage_in.at[stage, r],
                send_sem=s_send.at[stage], recv_sem=s_recv.at[stage],
                device_id=stage_peer(stage, r), device_id_type=MESH,
            ).start()
            return 0

        lax.fori_loop(1, 16, send, 0)
        if stage == 0:
            for w in range(2):
                coulomb_out[w] = jnp.sum(coulomb[w : w + 1])
                exchange_out[w] = jnp.sum(exchange[w : w + 1])
                weight_out[w] = jnp.sum(weight[w : w + 1])
        everyone = stage_in.at[stage, pl.ds(1, 15)]
        whole = pltpu.make_async_remote_copy(
            src_ref=everyone, dst_ref=everyone, send_sem=s_send.at[stage], recv_sem=s_recv.at[stage],
            device_id=sibling, device_id_type=MESH,
        )
        whole.wait_recv()
        whole.wait_send()
        group = None
        for a in range(16):
            term = stage_in[stage, lax.rem(me - a + 16, 16), 0:1, :]
            group = term if group is None else group + term
    share_out[...] = (GROUPS * group / jnp.sum(group, axis=1, keepdims=True))[:, 0:GROUPS]

    for copy in direct:
        copy.wait_send()
    for i in (5, 6):
        relay[i].wait_send()
    for i in range(7):
        share[i].wait_send()

    @pl.when(core == 0)
    def _():
        relay[7].wait_send()
        share[7].wait_send()

    for copy in g_copies:
        copy.wait_send()
    for copy in returns:
        copy.wait_send()


def local(greens, cholesky, fields, log_weight, group_of):
    f32, bf16 = jnp.float32, jnp.bfloat16
    dma = pltpu.SemaphoreType.DMA
    vmem = pl.BlockSpec(memory_space=pltpu.VMEM)
    smem = pl.BlockSpec(memory_space=pltpu.SMEM)
    hbm = pl.BlockSpec(memory_space=pl.ANY)
    bias, coulomb, exchange, weight, share = pl.pallas_call(
        kernel,
        out_shape=[
            jax.ShapeDtypeStruct((2, 176), f32),
            jax.ShapeDtypeStruct((2,), f32),
            jax.ShapeDtypeStruct((2,), f32),
            jax.ShapeDtypeStruct((2,), f32),
            jax.ShapeDtypeStruct((1, GROUPS), f32),
        ],
        in_specs=[hbm, hbm, vmem, smem, smem],
        out_specs=[vmem, smem, smem, smem, vmem],
        scratch_shapes=[
            pltpu.VMEM((44, 100, 1000), bf16),
            pltpu.VMEM((8, 2, 100, 1000), bf16),
            pltpu.VMEM((44 * ROWS, 1024), bf16),
            pltpu.VMEM((16, 128, 1024), bf16),
            pltpu.VMEM((11 * ROWS, 256), f32),
            pltpu.VMEM((11 * ROWS, 256), f32),
            pltpu.VMEM((16, 128, 128), f32),
            pltpu.VMEM((16, 8, 128), f32),
            pltpu.VMEM((8, 8, 256), f32),
            pltpu.VMEM((8, 8, 256), f32),
            pltpu.VMEM((4, 8, 256), f32),
            pltpu.VMEM((2, 8, 128), f32),
            pltpu.VMEM((2, 16, 8, 128), f32),
            dma((2,)),
            dma((16,)),
            dma((16,)),
            dma((7,)),
            dma((8,)),
            dma((8,)),
            dma((8,)),
            dma((2,)),
            dma((2,)),
        ],
        compiler_params=pltpu.CompilerParams(
            collective_id=0, has_side_effects=True, vmem_limit_bytes=56 * 2**20
        ),
        cost_estimate=pl.CostEstimate(flops=14_080_000_000, bytes_accessed=6_000_000, transcendentals=256),
    )(greens, cholesky, fields, log_weight, group_of)
    return bias, coulomb, exchange, weight, share.reshape(GROUPS)


def solution(mesh):
    in_specs = (
        P(("walk", "chol"), None, None, None),
        P("chol", None, None, None),
        P(("walk", "chol"), None),
        P(("walk", "chol")),
        P(("walk", "chol")),
    )
    out_specs = (
        P(("walk", "chol"), None),
        P(("walk", "chol")),
        P(("walk", "chol")),
        P(("walk", "chol")),
        P(),
    )
    return jax.shard_map(local, mesh=mesh, in_specs=in_specs, out_specs=out_specs, check_vma=False)
```

time: 447 us -> 108 us (0.24)
  waiting for transfers between devices: 163 us -> 0 us
  blocking collectives: 125 us -> 0 us
  Pallas kernels: 0 us -> 92.9 us
  matrix products: 42.9 us -> 0 us
  other arithmetic: 39.4 us -> 0 us
  local copies, waits for them, and re-layouts: 49.2 us -> 14 us
  between operations: 14.2 us -> 0.64 us
  starting transfers between devices: 11.7 us -> 0 us
    all_gather x2 -> x0, waiting for transfers between devices: 163 us -> none  [local(): lax.all_gather(members, 'chol', axis=0, tiled=True)]
    pallas_call x0 -> x1, Pallas kernels: none -> 92.9 us  [local(): pl.pallas_call(kernel, out_shape=[jax.ShapeDtypeStruct((2, 176), f32), ja...]
    psum x1 -> x0, blocking collectives: 89.2 us -> none  [local(): group_sums = lax.psum(local_sums, ('walk', 'chol'))]
    dot_general x3 -> x0, matrix products: 42.9 us -> none  [the longest x2 42.7 us: local(): jnp.einsum('gsip,wsjp->wgsij', cholesky, lax.all_gather(members, 'chol',...]
    unnamed x1 -> x0, blocking collectives: 36.1 us -> none
    unnamed x17 -> x7, local copies, waits for them, and re-layouts: 46.8 us -> 14 us
    dot_general x1 -> x0, other arithmetic: 23.9 us -> none  [local(): exch = jnp.einsum('wgsij,wgsji->w', prods, prods)]
    all_to_all x2 -> x0, starting transfers between devices: 11.6 us -> none  [local(): lax.all_to_all(bias, 'chol', split_axis=0, concat_axis=1, tiled=True)]
  transfers between devices with their start and end apart: 4 -> 0, of which waited for: 2 -> 0; matrix products, arithmetic and copies ran while one was open for 21% -> 0% of each run, Pallas kernels for 0% -> 0%
where the time goes in v1:
time: 108 us; the launch traced here: 107 us
  Pallas kernels  92.9 us (86%)
  local copies, waits for them, and re-layouts  14 us (13%)
    pallas_call x1, Pallas kernels, local(): pl.pallas_call(kernel, out_shape=[jax.ShapeDtypeStruct((2, 176), f32), ja...  92.9 us
    unnamed x7, local copies, waits for them, and re-layouts  14 us

profile of v1, /device:TPU:1, one launch (start us, length us, event | category | flops | bytes accessed | tf_op | source)
XLA Modules:
  0.0 107.5 jit_solution(456956666296873445)
XLA Ops:
  0.6 2.3 %copy.10.greens = bf16[2,2,100,1000]{3,2,1,0:T(8,128)(2,1)} copy(bf16[2,2,100,1000]{3,1,2,0:T(2,128)(2,1)} %param.5) | data formatting | bytes 1600000 | tf_op args[0]
  2.9 5.8 %copy.11.cholesky = bf16[11,2,100,1000]{3,2,1,0:T(8,128)(2,1)} copy(bf16[11,2,100,1000]{3,1,2,0:T(2,128)(2,1)} %param.6) | data formatting | bytes 8800000 | tf_op args[1]
  8.8 92.9 %shard_map.92 = (f32[2,176]{1,0:T(2,128)}, f32[2]{0:T(128)}, f32[2]{0:T(128)}, f32[2]{0:T(128)}, f32[1,16]{1,0:T(1,128)}) custom-call(bf16[2,2,100,1000]{3,2,1,0:T(8,128)(2,1)} %copy.10.greens, bf16[11,2,100,1000]{3,2,1,0:T(8,128)(2,1)} %copy.11.cholesky, f32[2,176]{1,0:T(2,128)} %fields.1, f32[2]{0:T(128)} %log_weight.1, s32[2]{0:T(128)} %group_of.1), custom_call_target="tpu_custom_call" | custom-call | flops 14080000000 | bytes 6000000 | tf_op jit(solution)/shard_map/pallas_call | solution.py:408
  101.6 1.2 %copy.17 = f32[2,176]{1,0:T(2,128)} copy(f32[2,176]{1,0:T(2,128)} %get-tuple-element.20) | data formatting | bytes 2816
  102.9 1.2 %copy.18 = f32[2]{0:T(128)} copy(f32[2]{0:T(128)} %get-tuple-element.21) | data formatting | bytes 16
  104.1 1.1 %copy.19 = f32[2]{0:T(128)} copy(f32[2]{0:T(128)} %get-tuple-element.22) | data formatting | bytes 16
  105.2 1.2 %copy.20 = f32[2]{0:T(128)} copy(f32[2]{0:T(128)} %get-tuple-element.23) | data formatting | bytes 16
  106.4 1.1 %copy.21 = f32[16]{0:T(128)} copy(f32[16]{0:T(128)} %bitcast.1) | data formatting | bytes 128

commit v2 on v0

v2 whole, which is shorter than its diff:
```python
import jax
import jax.numpy as jnp
import numpy as np
from jax import lax
from jax.experimental import pallas as pl
from jax.experimental.pallas import tpu as pltpu
from jax.sharding import PartitionSpec as P

GROUPS = 16
ROWS = 104
BLOCK = 11
MESH = pl.DeviceIdType.MESH
HIGHEST = lax.Precision.HIGHEST

SLOTS = ((0, 0), (1, 0), (0, -1), (0, 1), (1, -1), (0, 2), (1, 1), (1, -2))
WALKERS = (
    (0, 0), (0, 1), (1, 0), (2, 0), (3, 0), (1, 1), (2, 1), (3, 1),
    (4, 0), (5, 0), (4, 1), (5, 1), (6, 0), (7, 0), (6, 1), (7, 1),
)
QUARTERS = ((0, 1), (3, 6), (5, 7), (2, 4))

STEPS = (
    ((-1, 0), (1, 2)),
    ((-1, 1), (1, 3)),
    ((2, 0), (2, 2)),
    ((2, 1), (1, 0)),
    ((-1, 2), (1, 1)),
    ((-1, 3), (2, 3)),
)
ACROSS = ((0, 0), (0, 1), (1, 0), (2, 0), (2, 1), (3, 0), (3, 1), (4, 0), (4, 1))


def device(x, y, z, core):
    return {"walk": (y * 2 + lax.div(z, 4)) * 2 + core, "chol": lax.rem(z, 4) * 4 + x}


def kernel(
    greens, cholesky, fields, log_weight, group_of,
    bias_out, scalars_out, share_out,
    planes, walkers, prods_a, prods_b, bias_rows, exch, order,
    back, back_in, combined, stage_out, stage_in,
    local_sem, x_send, x_recv, near_send, near_recv, y_send, y_recv, far_recv,
    g_send, g_recv, b_send, b_recv, s_send, s_recv,
):
    wi, ci = lax.axis_index("walk"), lax.axis_index("chol")
    core = lax.rem(wi, 2)
    y = lax.div(wi, 4)
    z_lo = lax.div(ci, 4)
    z = lax.rem(lax.div(wi, 2), 2) * 4 + z_lo
    x = lax.rem(ci, 4)
    spin = lax.div(y, 2)
    mate = 3 - y
    odd = lax.rem(y, 2)
    neighbour = y + 1 - 2 * odd
    sends_across = core == odd

    def at_x(offset):
        return lax.rem(x + offset + 4, 4)

    def at_z(offset):
        return lax.rem(z + offset + 8, 8)

    def stage_peer(stage, r):
        if stage == 0:
            p = lax.rem(y * 4 + x + r, 16)
            return device(lax.rem(p, 4), lax.div(p, 4), z, core)
        p = lax.rem(z * 2 + core + r, 16)
        return device(x, y, lax.div(p, 2), lax.rem(p, 2))

    own_c = pltpu.make_async_copy(cholesky.at[:, spin], planes.at[pl.ds(0, 11)], local_sem.at[0])
    own_g = pltpu.make_async_copy(greens.at[:, spin], walkers.at[pl.ds(0, 2)], local_sem.at[1])
    own_g.start()
    own_c.start()

    barrier = pltpu.get_barrier_semaphore()

    def greet(peer):
        pl.semaphore_signal(barrier, inc=1, device_id=peer, device_id_type=MESH)

    for stage in range(2):
        def greet_stage(r, _, stage=stage):
            greet(stage_peer(stage, r))
            return 0
        lax.fori_loop(1, 16, greet_stage, 0)
    for offset in (-2, -1, 1, 2):
        greet(device(x, mate, at_z(offset), core))

    def plane_of(i, c):
        first = 3 * odd + 4 * c
        return first + odd + i if i < 3 else first + 3 * (1 - odd)

    def place(step, side, c):
        return BLOCK * (1 + step // 2) + (step % 2) * 4 + side * 2 + c

    def across_place(n):
        return BLOCK * (1 + n // 3) + 8 + n % 3

    lanes = lax.broadcasted_iota(jnp.int32, (1, 128), 1)
    rows = [(i, x * 11 + i) for i in range(11)]
    for step in range(6):
        for side in range(2):
            home, i = STEPS[step][side]
            for c in range(2):
                rows.append((place(step, side, c), at_x(home) * 11 + plane_of(i, c)))
    for n, (step, side) in enumerate(ACROSS):
        home, i = STEPS[step][side]
        rows.append((across_place(n), at_x(home) * 11 + 8 * (1 - odd) + i))
    rows.append((44, 44))
    order[...] = jnp.zeros_like(order)
    for at, row in rows:
        order[at : at + 1, :] = (lanes == row).astype(jnp.float32)
    bias_rows[...] = jnp.zeros_like(bias_rows)
    exch[...] = jnp.zeros_like(exch)
    prods_b[...] = jnp.zeros_like(prods_b)
    back[...] = jnp.zeros_like(back)
    pl.semaphore_wait(barrier, 34)

    sibling = device(x, y, z, 1 - core)
    to_side = (device(at_x(1), y, z, core), device(at_x(-1), y, z, core))

    def x_copy(step, side):
        home, i = STEPS[step][side]
        if home == 2:
            before = STEPS.index(next(s for s in STEPS if s[side] == ((-1, 1)[side], i)))
            src = planes.at[place(before, side, core)]
        else:
            src = cholesky.at[plane_of(i, core), spin]
        return pltpu.make_async_remote_copy(
            src_ref=src, dst_ref=planes.at[place(step, side, core)],
            send_sem=x_send.at[step, side], recv_sem=x_recv.at[step, side],
            device_id=to_side[side], device_id_type=MESH,
        )

    def near_copy(step, side, c):
        ref = planes.at[place(step, side, c)]
        return pltpu.make_async_remote_copy(
            src_ref=ref, dst_ref=ref, send_sem=near_send.at[step, side], recv_sem=near_recv.at[step, side],
            device_id=sibling, device_id_type=MESH,
        )

    def across_copy(n):
        step, side = ACROSS[n]
        return pltpu.make_async_remote_copy(
            src_ref=planes.at[place(step, side, core)], dst_ref=planes.at[across_place(n)],
            send_sem=y_send.at[n], recv_sem=y_recv.at[n],
            device_id=device(x, neighbour, z, core), device_id_type=MESH,
        )

    def onward_copy(n):
        ref = planes.at[across_place(n)]
        return pltpu.make_async_remote_copy(
            src_ref=ref, dst_ref=ref, send_sem=y_send.at[n], recv_sem=far_recv.at[n],
            device_id=sibling, device_id_type=MESH,
        )

    up, down = device(x, y, at_z(1), core), device(x, y, at_z(-1), core)

    def g_copy(slot, h):
        if slot < 4:
            src = greens.at[h, 1 - spin if slot == 1 else spin]
        else:
            src = walkers.at[WALKERS.index(({4: 1, 5: 3, 6: 1, 7: 4}[slot], h))]
        peer = device(x, mate, z, core) if slot == 1 else up if slot in (2, 4, 7) else down
        return pltpu.make_async_remote_copy(
            src_ref=src, dst_ref=walkers.at[WALKERS.index((slot, h))],
            send_sem=g_send.at[slot, h], recv_sem=g_recv.at[slot, h],
            device_id=peer, device_id_type=MESH,
        )

    def x_start(step):
        for side in range(2):
            x_copy(step, side).start()

    def x_arrived(step):
        for side in range(2):
            x_copy(step, side).wait_recv()
            near_copy(step, side, core).start()

        @pl.when(sends_across)
        def _():
            for n, (s, _side) in enumerate(ACROSS):
                if s == step:
                    across_copy(n).start()

    def across_arrived(numbers):
        @pl.when(jnp.logical_not(sends_across))
        def _():
            for n in numbers:
                across_copy(n).wait_recv()
                onward_copy(n).start()

    def block_whole(block):
        for step in (2 * block - 2, 2 * block - 1):
            for side in range(2):
                near_copy(step, side, 1 - core).wait_recv()

        @pl.when(sends_across)
        def _():
            for n in range(3 * block - 3, 3 * block):
                onward_copy(n).wait_recv()

    for step in range(2):
        g_copy(1, step).start()
        x_start(step)
        g_copy(2, step).start()
        g_copy(3, step).start()
    own_c.wait()
    own_g.wait()

    row = lax.broadcasted_iota(jnp.int32, (ROWS, 128), 0)
    col = lax.broadcasted_iota(jnp.int32, (ROWS, 128), 1)
    diagonal = row == col
    gap = jnp.zeros((28, 1000), jnp.bfloat16)

    def block_of(t):
        late = jnp.where(t < 18, 2, jnp.where(t < 24, lax.rem(t - 18, 3), 3))
        return jnp.where(t < 4, 0, jnp.where(t < 8, 1, jnp.where(t < 12, lax.rem(t, 2), late)))

    def pair_of(t):
        late = jnp.where(t < 18, t - 12, jnp.where(t < 24, 6 + lax.div(t - 18, 3), t - 24))
        return jnp.where(t < 4, t, jnp.where(t < 8, t - 4, jnp.where(t < 12, 4 + lax.div(t - 8, 2), late)))

    def product(t, buf):
        first, pair = block_of(t) * BLOCK, pair_of(t) * 2
        lhs = [part for i in range(BLOCK) for part in (planes[first + i], gap[: ROWS - 100])]
        rhs = [walkers[pair], gap, walkers[pair + 1], gap]
        buf[...] = lax.dot_general(
            jnp.concatenate(lhs, axis=0), jnp.concatenate(rhs, axis=0), (((1,), (1,)), ((), ())),
            preferred_element_type=jnp.float32,
        )

    def reduce(t, buf):
        first, pair = block_of(t) * BLOCK, pair_of(t) * 2
        for h in range(2):
            total = None
            for g in range(BLOCK):
                p = buf[g * ROWS : (g + 1) * ROWS, h * 128 : (h + 1) * 128]
                turned = p.T
                q = p[:, :ROWS] * turned[:ROWS, :]
                part = jnp.sum(q.reshape(ROWS // 8, 8, ROWS), axis=0)
                total = part if total is None else total + part
                d = jnp.sum(jnp.where(diagonal, p, 0.0).reshape(ROWS // 8, 8, 128), axis=0)
                bias_rows[pair + h, pl.ds(first + g, 1), :] = jnp.sum(d, axis=0, keepdims=True)
            exch[pair + h, :, 0:ROWS] += total

    def before(t, parity):
        def at(when, work):
            if when % 2 == parity:
                pl.when(t == when)(work)

        def walker(slot, h, *onward):
            g_copy(slot, h).wait_recv()
            for later in onward:
                g_copy(later, h).start()

        def first(h):
            x_arrived(h)
            x_start(h + 2)
            walker(3, h, 5)
            walker(1, h, 4)
            walker(2, h)

        def second():
            across_arrived((0, 1, 2))
            x_arrived(2)
            x_start(4)
            walker(4, 0, 7, 6)
            walker(5, 0)
            block_whole(1)

        def third():
            x_arrived(3)
            x_start(5)
            walker(4, 1, 7, 6)
            walker(5, 1)

        def fourth():
            across_arrived((3, 4, 5))
            block_whole(2)

        def fifth():
            walker(6, 0)
            walker(7, 0)

        def sixth():
            x_arrived(5)
            across_arrived((6, 7, 8))
            walker(6, 1)
            walker(7, 1)

        at(1, lambda: first(0))
        at(2, lambda: first(1))
        at(4, second)
        at(10, third)
        at(12, fourth)
        at(14, lambda: x_arrived(4))
        at(18, fifth)
        at(21, sixth)
        at(24, lambda: block_whole(3))

    def body(k, _):
        before(2 * k, 0)
        @pl.when(k>=0)
        def _():
            product(2 * k, prods_a)
            reduce(jnp.maximum(2 * k - 1, 0), prods_b)
        before(2 * k + 1, 1)
        @pl.when(k>=0)
        def _():
            product(2 * k + 1, prods_b)
            reduce(2 * k, prods_a)
        return 0

    lax.fori_loop(0, 16, body, 0)
    reduce(jnp.int32(31), prods_b)

    for w in range(16):
        bias_rows[w, 44:45, :] = jnp.sum(exch[w], axis=0, keepdims=True)
    sums = lax.dot_general(
        jnp.ones((8, 128), jnp.float32), bias_rows[...].reshape(16 * 128, 128), (((1,), (1,)), ((), ())),
        precision=HIGHEST, preferred_element_type=jnp.float32,
    )
    sums = jnp.concatenate([sums[0:1, w * 128 : (w + 1) * 128] for w in range(16)], axis=0)
    sums = jnp.dot(sums, order[...], precision=HIGHEST, preferred_element_type=jnp.float32)
    for slot in range(8):
        for h in range(2):
            w = WALKERS.index((slot, h))
            back[slot, h : h + 1] = sums[w : w + 1]
    returns = []
    for slot, (other, offset) in enumerate(SLOTS):
        if slot:
            copy = pltpu.make_async_remote_copy(
                src_ref=back.at[slot], dst_ref=back_in.at[slot], send_sem=b_send.at[slot], recv_sem=b_recv.at[slot],
                device_id=device(x, mate if other else y, at_z(offset), core), device_id_type=MESH,
            )
            copy.start()
            returns.append(copy)
    for copy in returns:
        copy.wait_recv()
    for quarter, (s, t) in enumerate(QUARTERS):
        combined[quarter] = (back[0] if s == 0 else back_in[s]) + back_in[t]
    lane = lax.broadcasted_iota(jnp.int32, (8, 128), 1)
    bias, exch_sum = None, None
    for m in range(4):
        block = combined[lax.rem(z_lo - m + 4, 4)]
        energy = jnp.sum(jnp.where(lane == 44, block, 0.0), axis=1, keepdims=True)
        wide = jnp.concatenate([jnp.where(lane < 44, block, 0.0), jnp.zeros((8, 128), jnp.float32)], axis=1)
        if m:
            wide = pltpu.roll(wide, 44 * m, 1)
        bias = wide if bias is None else bias + wide
        exch_sum = energy if exch_sum is None else exch_sum + energy
    bias, exch_sum = bias[0:2, 0:176], exch_sum[0:2]
    first = lax.broadcasted_iota(jnp.int32, (2, 1), 0) == 0
    root = np.sqrt(np.float32(176))
    coulomb = jnp.sum(bias * bias, axis=1, keepdims=True) / (2.0 * root)
    exchange = -exch_sum / (2.0 * root)
    importance = jnp.sum(fields[...] * bias - 0.5 * bias * bias, axis=1, keepdims=True) / root
    weight = jnp.where(first, log_weight[0], log_weight[1]) + importance - coulomb - exchange
    member = lax.broadcasted_iota(jnp.int32, (2, 128), 1) == jnp.where(
        lax.broadcasted_iota(jnp.int32, (2, 128), 0) == 0, group_of[0], group_of[1]
    )
    group = jnp.sum(jnp.where(member, jnp.exp(weight), 0.0), axis=0, keepdims=True)

    for stage in range(2):
        me = y * 4 + x if stage == 0 else z * 2 + core
        group = jnp.broadcast_to(group, (8, 128))
        stage_out[stage] = group
        stage_in[stage, 0] = group
        for r in range(1, 16):
            pltpu.make_async_remote_copy(
                src_ref=stage_out.at[stage], dst_ref=stage_in.at[stage, r],
                send_sem=s_send.at[stage], recv_sem=s_recv.at[stage],
                device_id=stage_peer(stage, r), device_id_type=MESH,
            ).start()
        if stage == 0:
            bias_out[...] = bias
            for w in range(2):
                scalars_out[w] = jnp.sum(coulomb[w : w + 1])
                scalars_out[2 + w] = jnp.sum(exchange[w : w + 1])
                scalars_out[4 + w] = jnp.sum(weight[w : w + 1])
        everyone = stage_in.at[stage, pl.ds(1, 15)]
        whole = pltpu.make_async_remote_copy(
            src_ref=everyone, dst_ref=everyone, send_sem=s_send.at[stage], recv_sem=s_recv.at[stage],
            device_id=sibling, device_id_type=MESH,
        )
        whole.wait_recv()
        whole.wait_send()
        group = None
        for a in range(16):
            term = stage_in[stage, lax.rem(me - a + 16, 16), 0:1, :]
            group = term if group is None else group + term
    share_out[...] = (GROUPS * group / jnp.sum(group, axis=1, keepdims=True))[:, 0:GROUPS]

    for step in range(6):
        for side in range(2):
            x_copy(step, side).wait_send()
            near_copy(step, side, core).wait_send()
    for n in range(9):
        across_copy(n).wait_send()
    for slot in range(1, 8):
        for h in range(2):
            g_copy(slot, h).wait_send()
    for copy in returns:
        copy.wait_send()


def hand_out(bias, scalars, share, bias_out, coulomb_out, exchange_out, weight_out, share_out):
    bias_out[...] = bias[...]
    share_out[...] = share[...]
    for w in range(2):
        coulomb_out[w] = scalars[w]
        exchange_out[w] = scalars[2 + w]
        weight_out[w] = scalars[4 + w]


def local(greens, cholesky, fields, log_weight, group_of):
    f32, bf16 = jnp.float32, jnp.bfloat16
    dma = pltpu.SemaphoreType.DMA
    vmem = pl.BlockSpec(memory_space=pltpu.VMEM)
    smem = pl.BlockSpec(memory_space=pltpu.SMEM)
    hbm = pl.BlockSpec(memory_space=pl.ANY)
    bias, scalars, share = pl.pallas_call(
        kernel,
        out_shape=[
            jax.ShapeDtypeStruct((2, 176), f32),
            jax.ShapeDtypeStruct((6,), f32),
            jax.ShapeDtypeStruct((1, GROUPS), f32),
        ],
        in_specs=[hbm, hbm, vmem, smem, smem],
        out_specs=[vmem, smem, vmem],
        scratch_shapes=[
            pltpu.VMEM((44, 100, 1000), bf16),
            pltpu.VMEM((16, 100, 1000), bf16),
            pltpu.VMEM((BLOCK * ROWS, 256), f32),
            pltpu.VMEM((BLOCK * ROWS, 256), f32),
            pltpu.VMEM((16, 128, 128), f32),
            pltpu.VMEM((16, 8, 128), f32),
            pltpu.VMEM((128, 128), f32),
            pltpu.VMEM((8, 8, 128), f32),
            pltpu.VMEM((8, 8, 128), f32),
            pltpu.VMEM((4, 8, 128), f32),
            pltpu.VMEM((2, 8, 128), f32),
            pltpu.VMEM((2, 16, 8, 128), f32),
            dma((2,)),
            dma((6, 2)),
            dma((6, 2)),
            dma((6, 2)),
            dma((6, 2)),
            dma((9,)),
            dma((9,)),
            dma((9,)),
            dma((8, 2)),
            dma((8, 2)),
            dma((8,)),
            dma((8,)),
            dma((2,)),
            dma((2,)),
        ],
        compiler_params=pltpu.CompilerParams(
            collective_id=0, has_side_effects=True, vmem_limit_bytes=56 * 2**20
        ),
        cost_estimate=pl.CostEstimate(flops=14_080_000_000, bytes_accessed=6_000_000, transcendentals=256),
    )(greens, cholesky, fields, log_weight, group_of)
    pair = jax.ShapeDtypeStruct((2,), f32)
    bias, coulomb, exchange, weight, share = pl.pallas_call(
        hand_out,
        out_shape=[bias, pair, pair, pair, share],
        in_specs=[vmem, smem, vmem],
        out_specs=[vmem, smem, smem, smem, vmem],
    )(bias, scalars, share)
    return bias, coulomb, exchange, weight, share.reshape(GROUPS)


def solution(mesh):
    in_specs = (
        P(("walk", "chol"), None, None, None),
        P("chol", None, None, None),
        P(("walk", "chol"), None),
        P(("walk", "chol")),
        P(("walk", "chol")),
    )
    out_specs = (
        P(("walk", "chol"), None),
        P(("walk", "chol")),
        P(("walk", "chol")),
        P(("walk", "chol")),
        P(),
    )
    return jax.shard_map(local, mesh=mesh, in_specs=in_specs, out_specs=out_specs, check_vma=False)
```

time: 447 us -> 88.1 us (0.20)
  waiting for transfers between devices: 163 us -> 0 us
  blocking collectives: 125 us -> 0 us
  Pallas kernels: 0 us -> 79.1 us
  matrix products: 42.9 us -> 0 us
  local copies, waits for them, and re-layouts: 49.2 us -> 8.13 us
  other arithmetic: 39.4 us -> 0 us
  between operations: 14.2 us -> 0.64 us
  starting transfers between devices: 11.7 us -> 0 us
    all_gather x2 -> x0, waiting for transfers between devices: 163 us -> none  [local(): lax.all_gather(members, 'chol', axis=0, tiled=True)]
    psum x1 -> x0, blocking collectives: 89.2 us -> none  [local(): group_sums = lax.psum(local_sums, ('walk', 'chol'))]
    pallas_call x0 -> x2, Pallas kernels: none -> 79.1 us  [the longest x1 77.7 us: local(): pl.pallas_call(kernel, out_shape=[jax.ShapeDtypeStruct((2, 176), f32), ja...]
    dot_general x3 -> x0, matrix products: 42.9 us -> none  [the longest x2 42.7 us: local(): jnp.einsum('gsip,wsjp->wgsij', cholesky, lax.all_gather(members, 'chol',...]
    unnamed x17 -> x2, local copies, waits for them, and re-layouts: 46.8 us -> 8.13 us
    unnamed x1 -> x0, blocking collectives: 36.1 us -> none
    dot_general x1 -> x0, other arithmetic: 23.9 us -> none  [local(): exch = jnp.einsum('wgsij,wgsji->w', prods, prods)]
    all_to_all x2 -> x0, starting transfers between devices: 11.6 us -> none  [local(): lax.all_to_all(bias, 'chol', split_axis=0, concat_axis=1, tiled=True)]
  transfers between devices with their start and end apart: 4 -> 0, of which waited for: 2 -> 0; matrix products, arithmetic and copies ran while one was open for 21% -> 0% of each run, Pallas kernels for 0% -> 0%
where the time goes in v2:
time: 88.1 us; the launch traced here: 87.9 us
  Pallas kernels  79.1 us (90%)
  local copies, waits for them, and re-layouts  8.13 us (9%)
    pallas_call x1, Pallas kernels, local(): pl.pallas_call(kernel, out_shape=[jax.ShapeDtypeStruct((2, 176), f32), ja...  77.7 us
    unnamed x2, local copies, waits for them, and re-layouts  8.13 us

profile of v2, /device:TPU:1, one launch (start us, length us, event | category | flops | bytes accessed | tf_op | source)
XLA Modules:
  0.0 87.9 jit_solution(968076049271542211)
XLA Ops:
  0.6 2.3 %copy.10.greens = bf16[2,2,100,1000]{3,2,1,0:T(8,128)(2,1)} copy(bf16[2,2,100,1000]{3,1,2,0:T(2,128)(2,1)} %param.5) | data formatting | bytes 1600000 | tf_op args[0]
  2.9 5.9 %copy.11.cholesky = bf16[11,2,100,1000]{3,2,1,0:T(8,128)(2,1)} copy(bf16[11,2,100,1000]{3,1,2,0:T(2,128)(2,1)} %param.6) | data formatting | bytes 8800000 | tf_op args[1]
  8.8 77.7 %shard_map.92 = (f32[2,176]{1,0:T(2,128)}, f32[6]{0:T(128)}, f32[1,16]{1,0:T(1,128)}) custom-call(bf16[2,2,100,1000]{3,2,1,0:T(8,128)(2,1)} %copy.10.greens, bf16[11,2,100,1000]{3,2,1,0:T(8,128)(2,1)} %copy.11.cholesky, f32[2,176]{1,0:T(2,128)} %fields.1, f32[2]{0:T(128)} %log_weight.1, s32[2]{0:T(128)} %group_of.1), custom_call_target="tpu_custom_call" | custom-call | flops 14080000000 | bytes 6000000 | tf_op jit(solution)/shard_map/pallas_call | solution.py:422
  86.5 1.4 %shard_map.93 = (f32[2,176]{1,0:T(2,128)}, f32[2]{0:T(128)}, f32[2]{0:T(128)}, f32[2]{0:T(128)}, f32[1,16]{1,0:T(1,128)}) custom-call(f32[2,176]{1,0:T(2,128)} %get-tuple-element.13.bias, f32[6]{0:T(128)} %get-tuple-element.14.scalars, f32[1,16]{1,0:T(1,128)} %get-tuple-element.15.share), custom_call_target="tpu_custom_call" | custom-call | tf_op jit(solution)/shard_map/pallas_call | solution.py:465

commit v3 on v2

--- a/solution.py
+++ b/solution.py
@@ -8,7 +8,8 @@
 
 GROUPS = 16
 ROWS = 104
-BLOCK = 11
+STREAM = 8
+PLANES = 44
 MESH = pl.DeviceIdType.MESH
 HIGHEST = lax.Precision.HIGHEST
 
@@ -21,13 +22,59 @@
 
 STEPS = (
     ((-1, 0), (1, 2)),
-    ((-1, 1), (1, 3)),
+    ((-1, 1), (1, 0)),
     ((2, 0), (2, 2)),
-    ((2, 1), (1, 0)),
-    ((-1, 2), (1, 1)),
+    ((-1, 2), (1, 3)),
+    ((2, 1), (1, 1)),
     ((-1, 3), (2, 3)),
 )
-ACROSS = ((0, 0), (0, 1), (1, 0), (2, 0), (2, 1), (3, 0), (3, 1), (4, 0), (4, 1))
+ACROSS = ((0, 0), (0, 1), (1, 0), (1, 1), (2, 0), (2, 1), (3, 0), (4, 0), (4, 1))
+FAR_FIRST = (
+    (10, 6, 14, 9, 11, 5, 7, 13, 15, 8, 2, 4, 12, 1, 3),
+    (8, 7, 9, 6, 10, 5, 11, 4, 12, 3, 13, 2, 14, 1, 15),
+)
+STEP_PLACE = (11, 15, 23, 27, 34, 40)
+ACROSS_PLACE = (19, 20, 21, 22, 31, 32, 33, 38, 39)
+
+
+def task_list():
+    walkers = PLANES
+
+    def early(*pairs):
+        return [(walkers, 2 * pair) for pair in pairs]
+
+    def blocks(numbers, *pairs):
+        return [(8 * number, walkers + 2 * pair) for pair in pairs for number in numbers]
+
+    tasks = blocks((0,), 0, 1, 2, 3) + early(4, 5, 6, 7, 8)
+    tasks += blocks((0, 1), 4) + early(9, 10, 11, 12) + blocks((2,), 4)
+    tasks += blocks((0, 1, 2), 5) + early(13, 14)
+    tasks += blocks((0, 1, 2), 6) + early(15, 16, 17, 18) + blocks((3,), 4, 5, 6)
+    tasks += blocks((0, 1, 2, 3), 7) + early(19, 20, 21) + blocks((4,), 4, 5, 6, 7)
+    return tasks + [(walkers + 8, 40), (walkers + 8, 42)]
+
+
+TASKS = task_list()
+
+
+def segments(values):
+    found, start = [], 0
+    while start < len(values):
+        end = start + 1
+        slope = values[end] - values[start] if end < len(values) else 0
+        while end < len(values) and values[end] == values[start] + slope * (end - start):
+            end += 1
+        found.append((end, start, values[start], slope))
+        start = end
+    return found
+
+
+def lookup(values, t):
+    result = None
+    for end, start, value, slope in reversed(segments(values)):
+        here = value + (t - start) * slope if slope else jnp.int32(value)
+        result = here if result is None else jnp.where(t < end, here, result)
+    return result
 
 
 def device(x, y, z, core):
@@ -37,7 +84,7 @@
 def kernel(
     greens, cholesky, fields, log_weight, group_of,
     bias_out, scalars_out, share_out,
-    planes, walkers, prods_a, prods_b, bias_rows, exch, order,
+    raw_c, raw_g, others, items, prods_a, prods_b, bias_rows, exch, order,
     back, back_in, combined, stage_out, stage_in,
     local_sem, x_send, x_recv, near_send, near_recv, y_send, y_recv, far_recv,
     g_send, g_recv, b_send, b_recv, s_send, s_recv,
@@ -67,8 +114,8 @@
         p = lax.rem(z * 2 + core + r, 16)
         return device(x, y, lax.div(p, 2), lax.rem(p, 2))
 
-    own_c = pltpu.make_async_copy(cholesky.at[:, spin], planes.at[pl.ds(0, 11)], local_sem.at[0])
-    own_g = pltpu.make_async_copy(greens.at[:, spin], walkers.at[pl.ds(0, 2)], local_sem.at[1])
+    own_c = pltpu.make_async_copy(cholesky, raw_c, local_sem.at[0])
+    own_g = pltpu.make_async_copy(greens, raw_g, local_sem.at[1])
     own_g.start()
     own_c.start()
 
@@ -90,10 +137,7 @@
         return first + odd + i if i < 3 else first + 3 * (1 - odd)
 
     def place(step, side, c):
-        return BLOCK * (1 + step // 2) + (step % 2) * 4 + side * 2 + c
-
-    def across_place(n):
-        return BLOCK * (1 + n // 3) + 8 + n % 3
+        return STEP_PLACE[step] + side * 2 + c
 
     lanes = lax.broadcasted_iota(jnp.int32, (1, 128), 1)
     rows = [(i, x * 11 + i) for i in range(11)]
@@ -104,8 +148,117 @@
                 rows.append((place(step, side, c), at_x(home) * 11 + plane_of(i, c)))
     for n, (step, side) in enumerate(ACROSS):
         home, i = STEPS[step][side]
-        rows.append((across_place(n), at_x(home) * 11 + 8 * (1 - odd) + i))
+        rows.append((ACROSS_PLACE[n], at_x(home) * 11 + 8 * (1 - odd) + i))
     rows.append((44, 44))
+    def by_spin(pair):
+        apart = jnp.swapaxes(pair, 0, 1)
+        low = spin == 0
+        return jnp.where(low, apart[0], apart[1]), jnp.where(low, apart[1], apart[0])
+
+    own_g.wait()
+    for h in range(2):
+        items[PLANES + h], others[h] = by_spin(raw_g[h])
+    own_c.wait()
+
+    def take(i, _):
+        items[i] = by_spin(raw_c[i])[0]
+        return 0
+
+    lax.fori_loop(0, 11, take, 0)
+    pl.semaphore_wait(barrier, 34)
+
+    sibling = device(x, y, z, 1 - core)
+    to_side = (device(at_x(1), y, z, core), device(at_x(-1), y, z, core))
+
+    def x_copy(step, side):
+        home, i = STEPS[step][side]
+        if home == 2:
+            before = STEPS.index(next(s for s in STEPS if s[side] == ((-1, 1)[side], i)))
+            src = items.at[place(before, side, core)]
+        else:
+            src = items.at[plane_of(i, core)]
+        return pltpu.make_async_remote_copy(
+            src_ref=src, dst_ref=items.at[place(step, side, core)],
+            send_sem=x_send.at[step, side], recv_sem=x_recv.at[step, side],
+            device_id=to_side[side], device_id_type=MESH,
+        )
+
+    def near_copy(step, side, c):
+        ref = items.at[place(step, side, c)]
+        return pltpu.make_async_remote_copy(
+            src_ref=ref, dst_ref=ref, send_sem=near_send.at[step, side], recv_sem=near_recv.at[step, side],
+            device_id=sibling, device_id_type=MESH,
+        )
+
+    def across_copy(n):
+        step, side = ACROSS[n]
+        return pltpu.make_async_remote_copy(
+            src_ref=items.at[place(step, side, core)], dst_ref=items.at[ACROSS_PLACE[n]],
+            send_sem=y_send.at[n], recv_sem=y_recv.at[n],
+            device_id=device(x, neighbour, z, core), device_id_type=MESH,
+        )
+
+    def onward_copy(n):
+        ref = items.at[ACROSS_PLACE[n]]
+        return pltpu.make_async_remote_copy(
+            src_ref=ref, dst_ref=ref, send_sem=y_send.at[n], recv_sem=far_recv.at[n],
+            device_id=sibling, device_id_type=MESH,
+        )
+
+    up, down = device(x, y, at_z(1), core), device(x, y, at_z(-1), core)
+
+    def g_copy(slot, h):
+        if slot < 4:
+            src = others.at[h] if slot == 1 else items.at[PLANES + h]
+        else:
+            src = items.at[PLANES + WALKERS.index(({4: 1, 5: 3, 6: 1, 7: 4}[slot], h))]
+        peer = device(x, mate, z, core) if slot == 1 else up if slot in (2, 4, 7) else down
+        return pltpu.make_async_remote_copy(
+            src_ref=src, dst_ref=items.at[PLANES + WALKERS.index((slot, h))],
+            send_sem=g_send.at[slot, h], recv_sem=g_recv.at[slot, h],
+            device_id=peer, device_id_type=MESH,
+        )
+
+    def x_start(step):
+        for side in range(2):
+            x_copy(step, side).start()
+
+    def x_arrived(step):
+        for side in range(2):
+            x_copy(step, side).wait_recv()
+            near_copy(step, side, core).start()
+
+        @pl.when(sends_across)
+        def _():
+            for n, (s, _side) in enumerate(ACROSS):
+                if s == step:
+                    across_copy(n).start()
+
+    def across_arrived(numbers):
+        @pl.when(jnp.logical_not(sends_across))
+        def _():
+            for n in numbers:
+                across_copy(n).wait_recv()
+                onward_copy(n).start()
+
+    def near_arrived(*steps):
+        for step in steps:
+            for side in range(2):
+                near_copy(step, side, 1 - core).wait_recv()
+
+    def onward_arrived(numbers):
+        @pl.when(sends_across)
+        def _():
+            for n in numbers:
+                onward_copy(n).wait_recv()
+
+    def begin(step):
+        g_copy(1, step).start()
+        x_start(step)
+        g_copy(2, step).start()
+        g_copy(3, step).start()
+
+    begin(0)
     order[...] = jnp.zeros_like(order)
     for at, row in rows:
         order[at : at + 1, :] = (lanes == row).astype(jnp.float32)
@@ -113,135 +266,37 @@
     exch[...] = jnp.zeros_like(exch)
     prods_b[...] = jnp.zeros_like(prods_b)
     back[...] = jnp.zeros_like(back)
-    pl.semaphore_wait(barrier, 34)
-
-    sibling = device(x, y, z, 1 - core)
-    to_side = (device(at_x(1), y, z, core), device(at_x(-1), y, z, core))
-
-    def x_copy(step, side):
-        home, i = STEPS[step][side]
-        if home == 2:
-            before = STEPS.index(next(s for s in STEPS if s[side] == ((-1, 1)[side], i)))
-            src = planes.at[place(before, side, core)]
-        else:
-            src = cholesky.at[plane_of(i, core), spin]
-        return pltpu.make_async_remote_copy(
-            src_ref=src, dst_ref=planes.at[place(step, side, core)],
-            send_sem=x_send.at[step, side], recv_sem=x_recv.at[step, side],
-            device_id=to_side[side], device_id_type=MESH,
-        )
-
-    def near_copy(step, side, c):
-        ref = planes.at[place(step, side, c)]
-        return pltpu.make_async_remote_copy(
-            src_ref=ref, dst_ref=ref, send_sem=near_send.at[step, side], recv_sem=near_recv.at[step, side],
-            device_id=sibling, device_id_type=MESH,
-        )
-
-    def across_copy(n):
-        step, side = ACROSS[n]
-        return pltpu.make_async_remote_copy(
-            src_ref=planes.at[place(step, side, core)], dst_ref=planes.at[across_place(n)],
-            send_sem=y_send.at[n], recv_sem=y_recv.at[n],
-            device_id=device(x, neighbour, z, core), device_id_type=MESH,
-        )
-
-    def onward_copy(n):
-        ref = planes.at[across_place(n)]
-        return pltpu.make_async_remote_copy(
-            src_ref=ref, dst_ref=ref, send_sem=y_send.at[n], recv_sem=far_recv.at[n],
-            device_id=sibling, device_id_type=MESH,
-        )
-
-    up, down = device(x, y, at_z(1), core), device(x, y, at_z(-1), core)
-
-    def g_copy(slot, h):
-        if slot < 4:
-            src = greens.at[h, 1 - spin if slot == 1 else spin]
-        else:
-            src = walkers.at[WALKERS.index(({4: 1, 5: 3, 6: 1, 7: 4}[slot], h))]
-        peer = device(x, mate, z, core) if slot == 1 else up if slot in (2, 4, 7) else down
-        return pltpu.make_async_remote_copy(
-            src_ref=src, dst_ref=walkers.at[WALKERS.index((slot, h))],
-            send_sem=g_send.at[slot, h], recv_sem=g_recv.at[slot, h],
-            device_id=peer, device_id_type=MESH,
-        )
-
-    def x_start(step):
-        for side in range(2):
-            x_copy(step, side).start()
-
-    def x_arrived(step):
-        for side in range(2):
-            x_copy(step, side).wait_recv()
-            near_copy(step, side, core).start()
-
-        @pl.when(sends_across)
-        def _():
-            for n, (s, _side) in enumerate(ACROSS):
-                if s == step:
-                    across_copy(n).start()
-
-    def across_arrived(numbers):
-        @pl.when(jnp.logical_not(sends_across))
-        def _():
-            for n in numbers:
-                across_copy(n).wait_recv()
-                onward_copy(n).start()
-
-    def block_whole(block):
-        for step in (2 * block - 2, 2 * block - 1):
-            for side in range(2):
-                near_copy(step, side, 1 - core).wait_recv()
-
-        @pl.when(sends_across)
-        def _():
-            for n in range(3 * block - 3, 3 * block):
-                onward_copy(n).wait_recv()
-
-    for step in range(2):
-        g_copy(1, step).start()
-        x_start(step)
-        g_copy(2, step).start()
-        g_copy(3, step).start()
-    own_c.wait()
-    own_g.wait()
 
     row = lax.broadcasted_iota(jnp.int32, (ROWS, 128), 0)
     col = lax.broadcasted_iota(jnp.int32, (ROWS, 128), 1)
     diagonal = row == col
     gap = jnp.zeros((28, 1000), jnp.bfloat16)
 
-    def block_of(t):
-        late = jnp.where(t < 18, 2, jnp.where(t < 24, lax.rem(t - 18, 3), 3))
-        return jnp.where(t < 4, 0, jnp.where(t < 8, 1, jnp.where(t < 12, lax.rem(t, 2), late)))
-
-    def pair_of(t):
-        late = jnp.where(t < 18, t - 12, jnp.where(t < 24, 6 + lax.div(t - 18, 3), t - 24))
-        return jnp.where(t < 4, t, jnp.where(t < 8, t - 4, jnp.where(t < 12, 4 + lax.div(t - 8, 2), late)))
+    def task(t):
+        return lookup([a for a, _ in TASKS], t), lookup([b for _, b in TASKS], t)
 
     def product(t, buf):
-        first, pair = block_of(t) * BLOCK, pair_of(t) * 2
-        lhs = [part for i in range(BLOCK) for part in (planes[first + i], gap[: ROWS - 100])]
-        rhs = [walkers[pair], gap, walkers[pair + 1], gap]
+        first, pair = task(t)
+        lhs = [part for i in range(STREAM) for part in (items[first + i], gap[: ROWS - 100])]
+        rhs = [items[pair], gap, items[pair + 1], gap]
         buf[...] = lax.dot_general(
             jnp.concatenate(lhs, axis=0), jnp.concatenate(rhs, axis=0), (((1,), (1,)), ((), ())),
             preferred_element_type=jnp.float32,
         )
 
     def reduce(t, buf):
-        first, pair = block_of(t) * BLOCK, pair_of(t) * 2
+        first, pair = task(t)
+        streams_walkers = first >= PLANES
         for h in range(2):
-            total = None
-            for g in range(BLOCK):
+            for g in range(STREAM):
+                walker = jnp.where(streams_walkers, first + g, pair + h) - PLANES
+                plane = jnp.where(streams_walkers, pair + h, first + g)
                 p = buf[g * ROWS : (g + 1) * ROWS, h * 128 : (h + 1) * 128]
                 turned = p.T
                 q = p[:, :ROWS] * turned[:ROWS, :]
-                part = jnp.sum(q.reshape(ROWS // 8, 8, ROWS), axis=0)
-                total = part if total is None else total + part
+                exch[walker, :, 0:ROWS] += jnp.sum(q.reshape(ROWS // 8, 8, ROWS), axis=0)
                 d = jnp.sum(jnp.where(diagonal, p, 0.0).reshape(ROWS // 8, 8, 128), axis=0)
-                bias_rows[pair + h, pl.ds(first + g, 1), :] = jnp.sum(d, axis=0, keepdims=True)
-            exch[pair + h, :, 0:ROWS] += total
+                bias_rows[walker, pl.ds(plane, 1), :] = jnp.sum(d, axis=0, keepdims=True)
 
     def before(t, parity):
         def at(when, work):
@@ -254,6 +309,8 @@
                 g_copy(later, h).start()
 
         def first(h):
+            if h == 0:
+                begin(1)
             x_arrived(h)
             x_start(h + 2)
             walker(3, h, 5)
@@ -261,58 +318,69 @@
             walker(2, h)
 
         def second():
-            across_arrived((0, 1, 2))
             x_arrived(2)
             x_start(4)
             walker(4, 0, 7, 6)
             walker(5, 0)
-            block_whole(1)
+            across_arrived((0, 1, 2, 3))
 
         def third():
+            near_arrived(2)
+            onward_arrived((0, 1, 2, 3))
+
+        def fourth():
             x_arrived(3)
             x_start(5)
             walker(4, 1, 7, 6)
             walker(5, 1)
 
-        def fourth():
-            across_arrived((3, 4, 5))
-            block_whole(2)
-
         def fifth():
+            x_arrived(4)
             walker(6, 0)
             walker(7, 0)
+            across_arrived((4, 5, 6))
 
         def sixth():
+            near_arrived(4)
+            onward_arrived((4, 5, 6))
+
+        def seventh():
             x_arrived(5)
-            across_arrived((6, 7, 8))
             walker(6, 1)
             walker(7, 1)
+            across_arrived((7, 8))
+
+        def eighth():
+            near_arrived(5)
+            onward_arrived((7, 8))
 
         at(1, lambda: first(0))
         at(2, lambda: first(1))
-        at(4, second)
-        at(10, third)
-        at(12, fourth)
-        at(14, lambda: x_arrived(4))
-        at(18, fifth)
-        at(21, sixth)
-        at(24, lambda: block_whole(3))
+        at(5, lambda: near_arrived(0, 1))
+        at(9, second)
+        at(11, third)
+        at(16, fourth)
+        at(19, lambda: near_arrived(3))
+        at(21, fifth)
+        at(24, sixth)
+        at(31, seventh)
+        at(35, eighth)
 
     def body(k, _):
         before(2 * k, 0)
-        @pl.when(k>=0)
+        @pl.when(k >= 0)
         def _():
             product(2 * k, prods_a)
             reduce(jnp.maximum(2 * k - 1, 0), prods_b)
         before(2 * k + 1, 1)
-        @pl.when(k>=0)
+        @pl.when(k >= 0)
         def _():
             product(2 * k + 1, prods_b)
             reduce(2 * k, prods_a)
         return 0
 
-    lax.fori_loop(0, 16, body, 0)
-    reduce(jnp.int32(31), prods_b)
+    lax.fori_loop(0, len(TASKS) // 2, body, 0)
+    reduce(jnp.int32(len(TASKS) - 1), prods_b)
 
     for w in range(16):
         bias_rows[w, 44:45, :] = jnp.sum(exch[w], axis=0, keepdims=True)
@@ -366,7 +434,7 @@
         group = jnp.broadcast_to(group, (8, 128))
         stage_out[stage] = group
         stage_in[stage, 0] = group
-        for r in range(1, 16):
+        for r in FAR_FIRST[stage]:
             pltpu.make_async_remote_copy(
                 src_ref=stage_out.at[stage], dst_ref=stage_in.at[stage, r],
                 send_sem=s_send.at[stage], recv_sem=s_recv.at[stage],
@@ -429,10 +497,12 @@
         in_specs=[hbm, hbm, vmem, smem, smem],
         out_specs=[vmem, smem, vmem],
         scratch_shapes=[
-            pltpu.VMEM((44, 100, 1000), bf16),
-            pltpu.VMEM((16, 100, 1000), bf16),
-            pltpu.VMEM((BLOCK * ROWS, 256), f32),
-            pltpu.VMEM((BLOCK * ROWS, 256), f32),
+            pltpu.VMEM((11, 100, 2, 1000), bf16),
+            pltpu.VMEM((2, 100, 2, 1000), bf16),
+            pltpu.VMEM((2, 100, 1000), bf16),
+            pltpu.VMEM((PLANES + 16, 100, 1000), bf16),
+            pltpu.VMEM((STREAM * ROWS, 256), f32),
+            pltpu.VMEM((STREAM * ROWS, 256), f32),
             pltpu.VMEM((16, 128, 128), f32),
             pltpu.VMEM((16, 8, 128), f32),
             pltpu.VMEM((128, 128), f32),
@@ -460,7 +530,7 @@
             collective_id=0, has_side_effects=True, vmem_limit_bytes=56 * 2**20
         ),
         cost_estimate=pl.CostEstimate(flops=14_080_000_000, bytes_accessed=6_000_000, transcendentals=256),
-    )(greens, cholesky, fields, log_weight, group_of)
+    )(jnp.transpose(greens, (0, 2, 1, 3)), jnp.transpose(cholesky, (0, 2, 1, 3)), fields, log_weight, group_of)
     pair = jax.ShapeDtypeStruct((2,), f32)
     bias, coulomb, exchange, weight, share = pl.pallas_call(
         hand_out,

time: 88.1 us -> 76.5 us (0.87)
  local copies, waits for them, and re-layouts: 8.13 us -> 0 us
  Pallas kernels: 79.1 us -> 75.7 us
    unnamed x2 -> x0, local copies, waits for them, and re-layouts: 8.13 us -> none
    pallas_call x1, Pallas kernels: 77.7 us -> 74.3 us  [local(): pl.pallas_call(kernel, out_shape=[jax.ShapeDtypeStruct((2, 176), f32), ja...]
where the time goes in v3:
time: 76.5 us; the launch traced here: 76.3 us
  Pallas kernels  75.7 us (99%)
    pallas_call x1, Pallas kernels, local(): pl.pallas_call(kernel, out_shape=[jax.ShapeDtypeStruct((2, 176), f32), ja...  74.3 us

profile of v3, /device:TPU:1, one launch (start us, length us, event | category | flops | bytes accessed | tf_op | source)
XLA Modules:
  0.0 76.3 jit_solution(1767602615600630152)
XLA Ops:
  0.6 74.3 %shard_map.92 = (f32[2,176]{1,0:T(2,128)}, f32[6]{0:T(128)}, f32[1,16]{1,0:T(1,128)}) custom-call(bf16[2,100,2,1000]{3,2,1,0:T(2,128)(2,1)} %bitcast.4, bf16[11,100,2,1000]{3,2,1,0:T(2,128)(2,1)} %bitcast.3, f32[2,176]{1,0:T(2,128)} %fields.1, f32[2]{0:T(128)} %log_weight.1, s32[2]{0:T(128)} %group_of.1), custom_call_target="tpu_custom_call" | custom-call | flops 14080000000 | bytes 6000000 | tf_op jit(solution)/shard_map/pallas_call | solution.py:490
  74.9 1.4 %shard_map.93 = (f32[2,176]{1,0:T(2,128)}, f32[2]{0:T(128)}, f32[2]{0:T(128)}, f32[2]{0:T(128)}, f32[1,16]{1,0:T(1,128)}) custom-call(f32[2,176]{1,0:T(2,128)} %get-tuple-element.13.bias, f32[6]{0:T(128)} %get-tuple-element.14.scalars, f32[1,16]{1,0:T(1,128)} %get-tuple-element.15.share), custom_call_target="tpu_custom_call" | custom-call | tf_op jit(solution)/shard_map/pallas_call | solution.py:535

commit v4 on v3

--- a/solution.py
+++ b/solution.py
@@ -29,10 +29,7 @@
     ((-1, 3), (2, 3)),
 )
 ACROSS = ((0, 0), (0, 1), (1, 0), (1, 1), (2, 0), (2, 1), (3, 0), (4, 0), (4, 1))
-FAR_FIRST = (
-    (10, 6, 14, 9, 11, 5, 7, 13, 15, 8, 2, 4, 12, 1, 3),
-    (8, 7, 9, 6, 10, 5, 11, 4, 12, 3, 13, 2, 14, 1, 15),
-)
+STAGES = ((4, 4), (8, 2))
 STEP_PLACE = (11, 15, 23, 27, 34, 40)
 ACROSS_PLACE = (19, 20, 21, 22, 31, 32, 33, 38, 39)
 
@@ -46,10 +43,10 @@
     def blocks(numbers, *pairs):
         return [(8 * number, walkers + 2 * pair) for pair in pairs for number in numbers]
 
-    tasks = blocks((0,), 0, 1, 2, 3) + early(4, 5, 6, 7, 8)
-    tasks += blocks((0, 1), 4) + early(9, 10, 11, 12) + blocks((2,), 4)
-    tasks += blocks((0, 1, 2), 5) + early(13, 14)
-    tasks += blocks((0, 1, 2), 6) + early(15, 16, 17, 18) + blocks((3,), 4, 5, 6)
+    tasks = blocks((0,), 0, 1, 2, 3) + early(4, 5, 6, 7, 8, 9)
+    tasks += blocks((0, 1), 4) + early(10, 11, 12) + blocks((2,), 4)
+    tasks += blocks((0, 1, 2), 5) + early(13, 14) + blocks((3,), 4)
+    tasks += blocks((0, 1, 2), 6) + early(15, 16, 17, 18) + blocks((3,), 5, 6)
     tasks += blocks((0, 1, 2, 3), 7) + early(19, 20, 21) + blocks((4,), 4, 5, 6, 7)
     return tasks + [(walkers + 8, 40), (walkers + 8, 42)]
 
@@ -84,7 +81,7 @@
 def kernel(
     greens, cholesky, fields, log_weight, group_of,
     bias_out, scalars_out, share_out,
-    raw_c, raw_g, others, items, prods_a, prods_b, bias_rows, exch, order,
+    raw_first, raw_c, raw_g, others, items, prods_a, prods_b, bias_rows, exch, order,
     back, back_in, combined, stage_out, stage_in,
     local_sem, x_send, x_recv, near_send, near_recv, y_send, y_recv, far_recv,
     g_send, g_recv, b_send, b_recv, s_send, s_recv,
@@ -107,16 +104,22 @@
     def at_z(offset):
         return lax.rem(z + offset + 8, 8)
 
-    def stage_peer(stage, r):
+    def stage_peer(stage, a, b):
         if stage == 0:
-            p = lax.rem(y * 4 + x + r, 16)
-            return device(lax.rem(p, 4), lax.div(p, 4), z, core)
-        p = lax.rem(z * 2 + core + r, 16)
-        return device(x, y, lax.div(p, 2), lax.rem(p, 2))
+            return device(xs[a], ys[b], z, core)
+        return device(x, y, zs[a], cores[b])
+
+    xs = [at_x(a) for a in range(4)]
+    ys = [lax.rem(y + b, 4) for b in range(4)]
+    zs = [at_z(a) for a in range(8)]
+    cores = [core, 1 - core]
 
     own_c = pltpu.make_async_copy(cholesky, raw_c, local_sem.at[0])
     own_g = pltpu.make_async_copy(greens, raw_g, local_sem.at[1])
+    first_plane = 3 * odd + 4 * core
+    first_c = pltpu.make_async_copy(cholesky.at[pl.ds(first_plane, 4)], raw_first, local_sem.at[2])
     own_g.start()
+    first_c.start()
     own_c.start()
 
     barrier = pltpu.get_barrier_semaphore()
@@ -124,13 +127,11 @@
     def greet(peer):
         pl.semaphore_signal(barrier, inc=1, device_id=peer, device_id_type=MESH)
 
-    for stage in range(2):
-        def greet_stage(r, _, stage=stage):
-            greet(stage_peer(stage, r))
-            return 0
-        lax.fori_loop(1, 16, greet_stage, 0)
-    for offset in (-2, -1, 1, 2):
-        greet(device(x, mate, at_z(offset), core))
+    sibling = device(x, y, z, 1 - core)
+    to_side = (device(at_x(1), y, z, core), device(at_x(-1), y, z, core))
+    up, down = device(x, y, at_z(1), core), device(x, y, at_z(-1), core)
+    for peer in (*to_side, up, down, sibling, device(x, neighbour, z, core), device(x, mate, z, core)):
+        greet(peer)
 
     def plane_of(i, c):
         first = 3 * odd + 4 * c
@@ -158,17 +159,10 @@
     own_g.wait()
     for h in range(2):
         items[PLANES + h], others[h] = by_spin(raw_g[h])
-    own_c.wait()
-
-    def take(i, _):
-        items[i] = by_spin(raw_c[i])[0]
-        return 0
-
-    lax.fori_loop(0, 11, take, 0)
-    pl.semaphore_wait(barrier, 34)
-
-    sibling = device(x, y, z, 1 - core)
-    to_side = (device(at_x(1), y, z, core), device(at_x(-1), y, z, core))
+    first_c.wait()
+    for i in range(4):
+        items[first_plane + i] = by_spin(raw_first[i])[0]
+    pl.semaphore_wait(barrier, 7)
 
     def x_copy(step, side):
         home, i = STEPS[step][side]
@@ -205,8 +199,6 @@
             device_id=sibling, device_id_type=MESH,
         )
 
-    up, down = device(x, y, at_z(1), core), device(x, y, at_z(-1), core)
-
     def g_copy(slot, h):
         if slot < 4:
             src = others.at[h] if slot == 1 else items.at[PLANES + h]
@@ -259,6 +251,15 @@
         g_copy(3, step).start()
 
     begin(0)
+    begin(1)
+    own_c.wait()
+
+    def take(i, _):
+        at = lax.rem(first_plane + 4 + i, 11)
+        items[at] = by_spin(raw_c[at])[0]
+        return 0
+
+    lax.fori_loop(0, 7, take, 0)
     order[...] = jnp.zeros_like(order)
     for at, row in rows:
         order[at : at + 1, :] = (lanes == row).astype(jnp.float32)
@@ -298,10 +299,9 @@
                 d = jnp.sum(jnp.where(diagonal, p, 0.0).reshape(ROWS // 8, 8, 128), axis=0)
                 bias_rows[walker, pl.ds(plane, 1), :] = jnp.sum(d, axis=0, keepdims=True)
 
-    def before(t, parity):
+    def before(t):
         def at(when, work):
-            if when % 2 == parity:
-                pl.when(t == when)(work)
+            pl.when(t == when)(work)
 
         def walker(slot, h, *onward):
             g_copy(slot, h).wait_recv()
@@ -309,8 +309,6 @@
                 g_copy(later, h).start()
 
         def first(h):
-            if h == 0:
-                begin(1)
             x_arrived(h)
             x_start(h + 2)
             walker(3, h, 5)
@@ -318,65 +316,71 @@
             walker(2, h)
 
         def second():
+            near_arrived(0, 1)
+            across_arrived((0,))
+
+        def third():
             x_arrived(2)
             x_start(4)
             walker(4, 0, 7, 6)
             walker(5, 0)
-            across_arrived((0, 1, 2, 3))
-
-        def third():
+            across_arrived((1, 2, 3))
+
+        def fourth():
             near_arrived(2)
-            onward_arrived((0, 1, 2, 3))
-
-        def fourth():
+            onward_arrived((1, 2, 3))
+
+        def fifth():
             x_arrived(3)
             x_start(5)
             walker(4, 1, 7, 6)
             walker(5, 1)
-
-        def fifth():
+            across_arrived((4,))
+
+        def sixth():
             x_arrived(4)
             walker(6, 0)
             walker(7, 0)
-            across_arrived((4, 5, 6))
-
-        def sixth():
+            across_arrived((5, 6))
+
+        def seventh():
             near_arrived(4)
-            onward_arrived((4, 5, 6))
-
-        def seventh():
+            onward_arrived((5, 6))
+
+        def eighth():
             x_arrived(5)
             walker(6, 1)
             walker(7, 1)
             across_arrived((7, 8))
 
-        def eighth():
+        def ninth():
             near_arrived(5)
             onward_arrived((7, 8))
 
-        at(1, lambda: first(0))
+        at(0, lambda: first(0))
         at(2, lambda: first(1))
-        at(5, lambda: near_arrived(0, 1))
-        at(9, second)
-        at(11, third)
-        at(16, fourth)
-        at(19, lambda: near_arrived(3))
-        at(21, fifth)
-        at(24, sixth)
-        at(31, seventh)
-        at(35, eighth)
+        at(4, second)
+        at(8, lambda: onward_arrived((0,)))
+        at(10, third)
+        at(12, fourth)
+        at(16, fifth)
+        at(18, lambda: near_arrived(3))
+        at(20, lambda: onward_arrived((4,)))
+        at(22, sixth)
+        at(24, seventh)
+        at(30, eighth)
+        at(34, ninth)
 
     def body(k, _):
-        before(2 * k, 0)
+        before(2 * k)
+
         @pl.when(k >= 0)
         def _():
             product(2 * k, prods_a)
             reduce(jnp.maximum(2 * k - 1, 0), prods_b)
-        before(2 * k + 1, 1)
-        @pl.when(k >= 0)
-        def _():
             product(2 * k + 1, prods_b)
             reduce(2 * k, prods_a)
+
         return 0
 
     lax.fori_loop(0, len(TASKS) // 2, body, 0)
@@ -430,15 +434,20 @@
     group = jnp.sum(jnp.where(member, jnp.exp(weight), 0.0), axis=0, keepdims=True)
 
     for stage in range(2):
-        me = y * 4 + x if stage == 0 else z * 2 + core
+        extent, other = STAGES[stage]
+        at, beside = (x, y) if stage == 0 else (z, core)
         group = jnp.broadcast_to(group, (8, 128))
         stage_out[stage] = group
         stage_in[stage, 0] = group
-        for r in FAR_FIRST[stage]:
+        far_first = sorted(
+            ((a, b) for a in range(extent) for b in range(other)),
+            key=lambda peer: -min(peer[0], extent - peer[0]) - min(peer[1], other - peer[1]),
+        )
+        for a, b in far_first[:-1]:
             pltpu.make_async_remote_copy(
-                src_ref=stage_out.at[stage], dst_ref=stage_in.at[stage, r],
+                src_ref=stage_out.at[stage], dst_ref=stage_in.at[stage, a + extent * b],
                 send_sem=s_send.at[stage], recv_sem=s_recv.at[stage],
-                device_id=stage_peer(stage, r), device_id_type=MESH,
+                device_id=stage_peer(stage, a, b), device_id_type=MESH,
             ).start()
         if stage == 0:
             bias_out[...] = bias
@@ -454,9 +463,12 @@
         whole.wait_recv()
         whole.wait_send()
         group = None
-        for a in range(16):
-            term = stage_in[stage, lax.rem(me - a + 16, 16), 0:1, :]
-            group = term if group is None else group + term
+        steps_a = [lax.rem(at - a + extent, extent) for a in range(extent)]
+        steps_b = [lax.rem(beside - b + other, other) * extent for b in range(other)]
+        for b in range(other):
+            for a in range(extent):
+                term = stage_in[stage, steps_a[a] + steps_b[b], 0:1, :]
+                group = term if group is None else group + term
     share_out[...] = (GROUPS * group / jnp.sum(group, axis=1, keepdims=True))[:, 0:GROUPS]
 
     for step in range(6):
@@ -497,6 +509,7 @@
         in_specs=[hbm, hbm, vmem, smem, smem],
         out_specs=[vmem, smem, vmem],
         scratch_shapes=[
+            pltpu.VMEM((4, 100, 2, 1000), bf16),
             pltpu.VMEM((11, 100, 2, 1000), bf16),
             pltpu.VMEM((2, 100, 2, 1000), bf16),
             pltpu.VMEM((2, 100, 1000), bf16),
@@ -511,7 +524,7 @@
             pltpu.VMEM((4, 8, 128), f32),
             pltpu.VMEM((2, 8, 128), f32),
             pltpu.VMEM((2, 16, 8, 128), f32),
-            dma((2,)),
+            dma((3,)),
             dma((6, 2)),
             dma((6, 2)),
             dma((6, 2)),

time: 76.5 us -> 74 us (0.967)
  Pallas kernels: 75.7 us -> 73.2 us
    pallas_call x1, Pallas kernels: 74.3 us -> 71.8 us  [local(): pl.pallas_call(kernel, out_shape=[jax.ShapeDtypeStruct((2, 176), f32), ja...]
where the time goes in v4:
time: 74 us; the launch traced here: 73.8 us
  Pallas kernels  73.2 us (99%)
    pallas_call x1, Pallas kernels, local(): pl.pallas_call(kernel, out_shape=[jax.ShapeDtypeStruct((2, 176), f32), ja...  71.8 us

profile of v4, /device:TPU:1, one launch (start us, length us, event | category | flops | bytes accessed | tf_op | source)
XLA Modules:
  0.0 73.8 jit_solution(16491389967158066990)
XLA Ops:
  0.6 71.8 %shard_map.92 = (f32[2,176]{1,0:T(2,128)}, f32[6]{0:T(128)}, f32[1,16]{1,0:T(1,128)}) custom-call(bf16[2,100,2,1000]{3,2,1,0:T(2,128)(2,1)} %bitcast.4, bf16[11,100,2,1000]{3,2,1,0:T(2,128)(2,1)} %bitcast.3, f32[2,176]{1,0:T(2,128)} %fields.1, f32[2]{0:T(128)} %log_weight.1, s32[2]{0:T(128)} %group_of.1), custom_call_target="tpu_custom_call" | custom-call | flops 14080000000 | bytes 6000000 | tf_op jit(solution)/shard_map/pallas_call | solution.py:502
  72.4 1.4 %shard_map.93 = (f32[2,176]{1,0:T(2,128)}, f32[2]{0:T(128)}, f32[2]{0:T(128)}, f32[2]{0:T(128)}, f32[1,16]{1,0:T(1,128)}) custom-call(f32[2,176]{1,0:T(2,128)} %get-tuple-element.13.bias, f32[6]{0:T(128)} %get-tuple-element.14.scalars, f32[1,16]{1,0:T(1,128)} %get-tuple-element.15.share), custom_call_target="tpu_custom_call" | custom-call | tf_op jit(solution)/shard_map/pallas_call | solution.py:548

commit v5 on v4

--- a/solution.py
+++ b/solution.py
@@ -34,6 +34,9 @@
 ACROSS_PLACE = (19, 20, 21, 22, 31, 32, 33, 38, 39)
 
 
+REPEATS = 30
+
+
 def task_list():
     walkers = PLANES
 
@@ -44,11 +47,12 @@
         return [(8 * number, walkers + 2 * pair) for pair in pairs for number in numbers]
 
     tasks = blocks((0,), 0, 1, 2, 3) + early(4, 5, 6, 7, 8, 9)
-    tasks += blocks((0, 1), 4) + early(10, 11, 12) + blocks((2,), 4)
-    tasks += blocks((0, 1, 2), 5) + early(13, 14) + blocks((3,), 4)
-    tasks += blocks((0, 1, 2), 6) + early(15, 16, 17, 18) + blocks((3,), 5, 6)
-    tasks += blocks((0, 1, 2, 3), 7) + early(19, 20, 21) + blocks((4,), 4, 5, 6, 7)
-    return tasks + [(walkers + 8, 40), (walkers + 8, 42)]
+    tasks += blocks((0, 1), 4) + early(10, 12, 11) + blocks((2,), 4)
+    tasks += blocks((0, 1, 2), 5) + early(13, 14) + blocks((3,), 4, 5) + early(15)
+    tasks += blocks((0, 1, 2), 6) + early(16, 17, 18) + blocks((3,), 6)
+    tasks += [(REPEATS, walkers + 2 * pair) for pair in (4, 5, 6)]
+    tasks += blocks((0, 1, 2, 3), 7) + [(REPEATS, walkers + 14)] + early(20, 21, 19)
+    return tasks + [(walkers + 8, 2 * pair) for pair in (20, 21, 19)]
 
 
 TASKS = task_list()
@@ -67,11 +71,14 @@
 
 
 def lookup(values, t):
-    result = None
-    for end, start, value, slope in reversed(segments(values)):
-        here = value + (t - start) * slope if slope else jnp.int32(value)
-        result = here if result is None else jnp.where(t < end, here, result)
-    return result
+    def pick(found):
+        if len(found) == 1:
+            _, start, value, slope = found[0]
+            return value + (t - start) * slope if slope else jnp.int32(value)
+        half = len(found) // 2
+        return jnp.where(t < found[half - 1][0], pick(found[:half]), pick(found[half:]))
+
+    return pick(segments(values))
 
 
 def device(x, y, z, core):
@@ -295,7 +302,10 @@
                 p = buf[g * ROWS : (g + 1) * ROWS, h * 128 : (h + 1) * 128]
                 turned = p.T
                 q = p[:, :ROWS] * turned[:ROWS, :]
-                exch[walker, :, 0:ROWS] += jnp.sum(q.reshape(ROWS // 8, 8, ROWS), axis=0)
+                part = jnp.sum(q.reshape(ROWS // 8, 8, ROWS), axis=0)
+                if g < 2:
+                    part = jnp.where(first == REPEATS, 0.0, part)
+                exch[walker, :, 0:ROWS] += part
                 d = jnp.sum(jnp.where(diagonal, p, 0.0).reshape(ROWS // 8, 8, 128), axis=0)
                 bias_rows[walker, pl.ds(plane, 1), :] = jnp.sum(d, axis=0, keepdims=True)
 
@@ -324,11 +334,12 @@
             x_start(4)
             walker(4, 0, 7, 6)
             walker(5, 0)
-            across_arrived((1, 2, 3))
+            across_arrived((1, 2))
 
         def fourth():
             near_arrived(2)
-            onward_arrived((1, 2, 3))
+            onward_arrived((1, 2))
+            across_arrived((3,))
 
         def fifth():
             x_arrived(3)
@@ -351,25 +362,34 @@
             x_arrived(5)
             walker(6, 1)
             walker(7, 1)
-            across_arrived((7, 8))
-
-        def ninth():
-            near_arrived(5)
-            onward_arrived((7, 8))
-
-        at(0, lambda: first(0))
-        at(2, lambda: first(1))
-        at(4, second)
-        at(8, lambda: onward_arrived((0,)))
-        at(10, third)
-        at(12, fourth)
-        at(16, fifth)
-        at(18, lambda: near_arrived(3))
-        at(20, lambda: onward_arrived((4,)))
-        at(22, sixth)
-        at(24, seventh)
-        at(30, eighth)
-        at(34, ninth)
+
+        @pl.when(t < 10)
+        def _():
+            at(0, lambda: first(0))
+            at(2, lambda: first(1))
+            at(4, second)
+            at(8, lambda: onward_arrived((0,)))
+
+        @pl.when(jnp.logical_and(t >= 10, t < 20))
+        def _():
+            at(10, third)
+            at(12, fourth)
+            at(14, lambda: onward_arrived((3,)))
+            at(16, fifth)
+            at(18, lambda: near_arrived(3))
+
+        @pl.when(jnp.logical_and(t >= 20, t < 28))
+        def _():
+            at(20, lambda: onward_arrived((4,)))
+            at(24, sixth)
+            at(26, seventh)
+
+        @pl.when(t >= 34)
+        def _():
+            at(34, eighth)
+            at(36, lambda: across_arrived((7, 8)))
+            at(38, lambda: near_arrived(5))
+            at(40, lambda: onward_arrived((7, 8)))
 
     def body(k, _):
         before(2 * k)
@@ -384,22 +404,22 @@
         return 0
 
     lax.fori_loop(0, len(TASKS) // 2, body, 0)
-    reduce(jnp.int32(len(TASKS) - 1), prods_b)
+    product(jnp.int32(len(TASKS) - 1), prods_a)
+    reduce(jnp.int32(len(TASKS) - 2), prods_b)
+    reduce(jnp.int32(len(TASKS) - 1), prods_a)
 
     for w in range(16):
         bias_rows[w, 44:45, :] = jnp.sum(exch[w], axis=0, keepdims=True)
-    sums = lax.dot_general(
-        jnp.ones((8, 128), jnp.float32), bias_rows[...].reshape(16 * 128, 128), (((1,), (1,)), ((), ())),
+    wide = jnp.dot(
+        bias_rows[...].reshape(16 * 48, 128), jnp.ones((128, 128), jnp.float32),
         precision=HIGHEST, preferred_element_type=jnp.float32,
-    )
-    sums = jnp.concatenate([sums[0:1, w * 128 : (w + 1) * 128] for w in range(16)], axis=0)
-    sums = jnp.dot(sums, order[...], precision=HIGHEST, preferred_element_type=jnp.float32)
+    ).reshape(16, 48, 128)
+    sums = [jnp.sum(wide[w] * order[...], axis=0, keepdims=True) for w in range(16)]
     for slot in range(8):
         for h in range(2):
-            w = WALKERS.index((slot, h))
-            back[slot, h : h + 1] = sums[w : w + 1]
+            back[slot, h : h + 1] = sums[WALKERS.index((slot, h))]
     returns = []
-    for slot, (other, offset) in enumerate(SLOTS):
+    for slot, (other, offset) in reversed(tuple(enumerate(SLOTS))):
         if slot:
             copy = pltpu.make_async_remote_copy(
                 src_ref=back.at[slot], dst_ref=back_in.at[slot], send_sem=b_send.at[slot], recv_sem=b_recv.at[slot],
@@ -516,9 +536,9 @@
             pltpu.VMEM((PLANES + 16, 100, 1000), bf16),
             pltpu.VMEM((STREAM * ROWS, 256), f32),
             pltpu.VMEM((STREAM * ROWS, 256), f32),
-            pltpu.VMEM((16, 128, 128), f32),
+            pltpu.VMEM((16, 48, 128), f32),
             pltpu.VMEM((16, 8, 128), f32),
-            pltpu.VMEM((128, 128), f32),
+            pltpu.VMEM((48, 128), f32),
             pltpu.VMEM((8, 8, 128), f32),
             pltpu.VMEM((8, 8, 128), f32),
             pltpu.VMEM((4, 8, 128), f32),

time: 74 us -> 71.3 us (0.964)
  Pallas kernels: 73.2 us -> 70.6 us
    pallas_call x1, Pallas kernels: 71.8 us -> 69.2 us  [local(): pl.pallas_call(kernel, out_shape=[jax.ShapeDtypeStruct((2, 176), f32), ja...]
where the time goes in v5:
time: 71.3 us; the launch traced here: 71.2 us
  Pallas kernels  70.6 us (99%)
    pallas_call x1, Pallas kernels, local(): pl.pallas_call(kernel, out_shape=[jax.ShapeDtypeStruct((2, 176), f32), ja...  69.2 us

profile of v5, /device:TPU:1, one launch (start us, length us, event | category | flops | bytes accessed | tf_op | source)
XLA Modules:
  0.0 71.2 jit_solution(8129026975364561688)
XLA Ops:
  0.6 69.2 %shard_map.92 = (f32[2,176]{1,0:T(2,128)}, f32[6]{0:T(128)}, f32[1,16]{1,0:T(1,128)}) custom-call(bf16[2,100,2,1000]{3,2,1,0:T(2,128)(2,1)} %bitcast.4, bf16[11,100,2,1000]{3,2,1,0:T(2,128)(2,1)} %bitcast.3, f32[2,176]{1,0:T(2,128)} %fields.1, f32[2]{0:T(128)} %log_weight.1, s32[2]{0:T(128)} %group_of.1), custom_call_target="tpu_custom_call" | custom-call | flops 14080000000 | bytes 6000000 | tf_op jit(solution)/shard_map/pallas_call | solution.py:522
  69.8 1.4 %shard_map.93 = (f32[2,176]{1,0:T(2,128)}, f32[2]{0:T(128)}, f32[2]{0:T(128)}, f32[2]{0:T(128)}, f32[1,16]{1,0:T(1,128)}) custom-call(f32[2,176]{1,0:T(2,128)} %get-tuple-element.13.bias, f32[6]{0:T(128)} %get-tuple-element.14.scalars, f32[1,16]{1,0:T(1,128)} %get-tuple-element.15.share), custom_call_target="tpu_custom_call" | custom-call | tf_op jit(solution)/shard_map/pallas_call | solution.py:568

commit v6 on v5

--- a/solution.py
+++ b/solution.py
@@ -363,43 +363,48 @@
             walker(6, 1)
             walker(7, 1)
 
-        @pl.when(t < 10)
-        def _():
-            at(0, lambda: first(0))
-            at(2, lambda: first(1))
-            at(4, second)
-            at(8, lambda: onward_arrived((0,)))
-
-        @pl.when(jnp.logical_and(t >= 10, t < 20))
-        def _():
-            at(10, third)
-            at(12, fourth)
-            at(14, lambda: onward_arrived((3,)))
-            at(16, fifth)
-            at(18, lambda: near_arrived(3))
-
-        @pl.when(jnp.logical_and(t >= 20, t < 28))
-        def _():
-            at(20, lambda: onward_arrived((4,)))
-            at(24, sixth)
-            at(26, seventh)
-
-        @pl.when(t >= 34)
-        def _():
-            at(34, eighth)
-            at(36, lambda: across_arrived((7, 8)))
-            at(38, lambda: near_arrived(5))
-            at(40, lambda: onward_arrived((7, 8)))
+        def split(when, early, late):
+            lax.cond(t < when, early, late)
+
+        def run(*work):
+            def go():
+                for when, what in work:
+                    at(when, what)
+            return go
+
+        split(
+            16,
+            lambda: split(
+                6,
+                run((0, lambda: first(0)), (2, lambda: first(1)), (4, second)),
+                lambda: split(
+                    12,
+                    run((8, lambda: onward_arrived((0,))), (10, third)),
+                    run((12, fourth), (14, lambda: onward_arrived((3,)))),
+                ),
+            ),
+            lambda: split(
+                28,
+                lambda: split(
+                    22,
+                    run((16, fifth), (18, lambda: near_arrived(3)), (20, lambda: onward_arrived((4,)))),
+                    run((24, sixth), (26, seventh)),
+                ),
+                lambda: split(
+                    38,
+                    run((34, eighth), (36, lambda: across_arrived((7, 8)))),
+                    run((38, lambda: near_arrived(5)), (40, lambda: onward_arrived((7, 8)))),
+                ),
+            ),
+        )
 
     def body(k, _):
         before(2 * k)
 
-        @pl.when(k >= 0)
-        def _():
-            product(2 * k, prods_a)
-            reduce(jnp.maximum(2 * k - 1, 0), prods_b)
-            product(2 * k + 1, prods_b)
-            reduce(2 * k, prods_a)
+        product(2 * k, prods_a)
+        reduce(jnp.maximum(2 * k - 1, 0), prods_b)
+        product(2 * k + 1, prods_b)
+        reduce(2 * k, prods_a)
 
         return 0
 

time: 71.3 us -> 70.6 us (level)
  Pallas kernels: 70.6 us -> 69.8 us
    pallas_call x1, Pallas kernels: 69.2 us -> 68.5 us  [local(): pl.pallas_call(kernel, out_shape=[jax.ShapeDtypeStruct((2, 176), f32), ja...]
where the time goes in v6:
time: 70.6 us; the launch traced here: 70.5 us
  Pallas kernels  69.8 us (99%)
    pallas_call x1, Pallas kernels, local(): pl.pallas_call(kernel, out_shape=[jax.ShapeDtypeStruct((2, 176), f32), ja...  68.5 us

profile of v6, /device:TPU:1, one launch (start us, length us, event | category | flops | bytes accessed | tf_op | source)
XLA Modules:
  0.0 70.5 jit_solution(6231452826562496796)
XLA Ops:
  0.6 68.5 %shard_map.92 = (f32[2,176]{1,0:T(2,128)}, f32[6]{0:T(128)}, f32[1,16]{1,0:T(1,128)}) custom-call(bf16[2,100,2,1000]{3,2,1,0:T(2,128)(2,1)} %bitcast.4, bf16[11,100,2,1000]{3,2,1,0:T(2,128)(2,1)} %bitcast.3, f32[2,176]{1,0:T(2,128)} %fields.1, f32[2]{0:T(128)} %log_weight.1, s32[2]{0:T(128)} %group_of.1), custom_call_target="tpu_custom_call" | custom-call | flops 14080000000 | bytes 6000000 | tf_op jit(solution)/shard_map/pallas_call | solution.py:527
  69.1 1.4 %shard_map.93 = (f32[2,176]{1,0:T(2,128)}, f32[2]{0:T(128)}, f32[2]{0:T(128)}, f32[2]{0:T(128)}, f32[1,16]{1,0:T(1,128)}) custom-call(f32[2,176]{1,0:T(2,128)} %get-tuple-element.13.bias, f32[6]{0:T(128)} %get-tuple-element.14.scalars, f32[1,16]{1,0:T(1,128)} %get-tuple-element.15.share), custom_call_target="tpu_custom_call" | custom-call | tf_op jit(solution)/shard_map/pallas_call | solution.py:573

commit v7 on v6

--- a/solution.py
+++ b/solution.py
@@ -275,9 +275,10 @@
     prods_b[...] = jnp.zeros_like(prods_b)
     back[...] = jnp.zeros_like(back)
 
-    row = lax.broadcasted_iota(jnp.int32, (ROWS, 128), 0)
-    col = lax.broadcasted_iota(jnp.int32, (ROWS, 128), 1)
-    diagonal = row == col
+    row = lax.broadcasted_iota(jnp.int32, (8, 128), 0)
+    col = lax.broadcasted_iota(jnp.int32, (8, 128), 1)
+    tile = lax.div(col, 8)
+    diagonal = jnp.logical_and(row == lax.rem(col, 8), col < ROWS)
     gap = jnp.zeros((28, 1000), jnp.bfloat16)
 
     def task(t):
@@ -306,7 +307,10 @@
                 if g < 2:
                     part = jnp.where(first == REPEATS, 0.0, part)
                 exch[walker, :, 0:ROWS] += part
-                d = jnp.sum(jnp.where(diagonal, p, 0.0).reshape(ROWS // 8, 8, 128), axis=0)
+                d = p[0:8]
+                for r in range(1, ROWS // 8):
+                    d = jnp.where(tile == r, p[r * 8 : r * 8 + 8], d)
+                d = jnp.where(diagonal, d, 0.0)
                 bias_rows[walker, pl.ds(plane, 1), :] = jnp.sum(d, axis=0, keepdims=True)
 
     def before(t):

time: 70.6 us -> 70.6 us (level)
  no operation moved by 1% of the time
where the time goes in v7:
time: 70.6 us; the launch traced here: 70.5 us
  Pallas kernels  69.8 us (99%)
    pallas_call x1, Pallas kernels, local(): pl.pallas_call(kernel, out_shape=[jax.ShapeDtypeStruct((2, 176), f32), ja...  68.4 us

profile of v7, /device:TPU:1, one launch (start us, length us, event | category | flops | bytes accessed | tf_op | source)
XLA Modules:
  0.0 70.5 jit_solution(4509344543406492243)
XLA Ops:
  0.6 68.4 %shard_map.92 = (f32[2,176]{1,0:T(2,128)}, f32[6]{0:T(128)}, f32[1,16]{1,0:T(1,128)}) custom-call(bf16[2,100,2,1000]{3,2,1,0:T(2,128)(2,1)} %bitcast.4, bf16[11,100,2,1000]{3,2,1,0:T(2,128)(2,1)} %bitcast.3, f32[2,176]{1,0:T(2,128)} %fields.1, f32[2]{0:T(128)} %log_weight.1, s32[2]{0:T(128)} %group_of.1), custom_call_target="tpu_custom_call" | custom-call | flops 14080000000 | bytes 6000000 | tf_op jit(solution)/shard_map/pallas_call | solution.py:531
  69.1 1.4 %shard_map.93 = (f32[2,176]{1,0:T(2,128)}, f32[2]{0:T(128)}, f32[2]{0:T(128)}, f32[2]{0:T(128)}, f32[1,16]{1,0:T(1,128)}) custom-call(f32[2,176]{1,0:T(2,128)} %get-tuple-element.13.bias, f32[6]{0:T(128)} %get-tuple-element.14.scalars, f32[1,16]{1,0:T(1,128)} %get-tuple-element.15.share), custom_call_target="tpu_custom_call" | custom-call | tf_op jit(solution)/shard_map/pallas_call | solution.py:577
